TPU v7x, 32 devices: a whole 2x2x4 slice. The times are simulated.
32 devices in a mesh: batch: 16 (over z, y, x), head: 2 (over core).
Axes of the slice: x: 2, y: 2, z: 4, core: 2. Of those that a mesh axis runs over, the one named last changes fastest.
Arguments:
- tokens: bfloat16 [32, 197, 768], P(('batch', 'head')), may hold values from -6 to 6
- kept_index: int32 [32, 196], P(('batch', 'head')), may hold values from 0 to 195, as said below
- kept_count: int32 [32], P(('batch', 'head')), may hold values from 79 to 196
- prompts: bfloat16 [50, 768], replicated, may hold values from -6 to 6
- gain_one: bfloat16 [768], replicated, may hold values from 0.3984375 to 1.59375
- shift_one: bfloat16 [768], replicated, may hold values from -1.5 to 1.5
- w_query: bfloat16 [768, 768], P(None, 'head'), may hold values from -0.21875 to 0.21875
- b_query: bfloat16 [768], P('head'), may hold values from -1.5 to 1.5
- w_key: bfloat16 [768, 768], P(None, 'head'), may hold values from -0.21875 to 0.21875
- w_value: bfloat16 [768, 768], P(None, 'head'), may hold values from -0.21875 to 0.21875
- b_value: bfloat16 [768], P('head'), may hold values from -1.5 to 1.5
- w_out: bfloat16 [768, 768], P('head'), may hold values from -1.5 to 1.5
- b_out: bfloat16 [768], replicated, may hold values from -1.5 to 1.5
- gain_two: bfloat16 [768], replicated, may hold values from 0.3984375 to 1.59375
- shift_two: bfloat16 [768], replicated, may hold values from -1.5 to 1.5
- w_fc1: bfloat16 [3072, 768], P(('batch', 'head')), may hold values from -0.21875 to 0.21875
- b_fc1: bfloat16 [3072], P(('batch', 'head')), may hold values from -1.5 to 1.5
- w_fc2: bfloat16 [3072, 768], P(('batch', 'head')), may hold values from -0.109375 to 0.109375
- b_fc2: bfloat16 [768], replicated, may hold values from -1.5 to 1.5
- cotangent: bfloat16 [32, 256, 768], P(('batch', 'head')), may hold values from -6 to 6
Outputs:
- layer_out: bfloat16 [32, 256, 768], P(('batch', 'head'))
- grad_tokens: float32 [32, 197, 768], P(('batch', 'head'))
- grad_prompts: float32 [50, 768], replicated
- grad_gain_one: float32 [768], replicated
- grad_shift_one: float32 [768], replicated
- grad_w_query: float32 [768, 768], P(None, 'head')
- grad_b_query: float32 [768], P('head')
- grad_w_key: float32 [768, 768], P(None, 'head')
- grad_w_value: float32 [768, 768], P(None, 'head')
- grad_b_value: float32 [768], P('head')
- grad_w_out: float32 [768, 768], P('head')
- grad_b_out: float32 [768], replicated
- grad_gain_two: float32 [768], replicated
- grad_shift_two: float32 [768], replicated
- grad_w_fc1: float32 [3072, 768], P(('batch', 'head'))
- grad_b_fc1: float32 [3072], P(('batch', 'head'))
- grad_w_fc2: float32 [3072, 768], P(('batch', 'head'))
- grad_b_fc2: float32 [768], replicated
Inputs may be any that keep to these rules, and one draw needn't show every extreme that they name: `kept_index`: row i holds kept_count[i] different patch numbers in rising order, then zeros.
All inputs are finite; a program needn't handle non-finite values.
Results may differ from a plain program's by a relative error of at most 0.013.
Values may be sent and summed in bfloat16 or wider, within the bound.
A program may use at most 128 MiB of HBM per device.

v0:
```python
from functools import partial
import math

import jax
import jax.numpy as jnp
from jax import lax
from jax.sharding import PartitionSpec as P

HEAD_DIM = 64


EPSILON = 1e-06


def layer_norm(rows_in, gain_vec, shift_vec):
    centre = jnp.mean(rows_in, axis=-1, keepdims=True)
    centred = rows_in - centre
    spread = jnp.mean(centred * centred, axis=-1, keepdims=True)
    return centred * lax.rsqrt(spread + EPSILON) * gain_vec + shift_vec


def selector(kept_index, kept_count, column_count, offset):
    patch_count = kept_index.shape[1]
    slot_ids = jnp.arange(patch_count, dtype=jnp.int32)
    slot_live = slot_ids[None, :] < kept_count[:, None]
    columns = jnp.arange(column_count, dtype=jnp.int32)
    hits = (kept_index + offset)[:, :, None] == columns[None, None, :]
    return hits & slot_live[:, :, None]


def assemble(tokens, prompts, kept_index, kept_count, seq_rows):
    image_count = tokens.shape[0]
    model_width = tokens.shape[2]
    patch_count = kept_index.shape[1]
    prompt_count = prompts.shape[0]
    picker = selector(kept_index, kept_count, tokens.shape[1], 1).astype(jnp.bfloat16)
    picked = jnp.einsum("bij,bjd->bid", picker, tokens, preferred_element_type=jnp.float32)
    leading = tokens[:, 0:1, :].astype(jnp.float32)
    prompt_rows = prompts.astype(jnp.float32)[None, :, :]
    padding = jnp.zeros(
        (image_count, seq_rows - 1 - prompt_count - patch_count, model_width), jnp.float32
    )
    return jnp.concatenate([leading, prompt_rows, picked, padding], axis=1)


def contract_rows(left, right):
    return lax.dot_general(
        left, right, (((0,), (0,)), ((), ())), preferred_element_type=jnp.float32
    )


def contract_cols(left, right):
    return lax.dot_general(
        left, right, (((1,), (1,)), ((), ())), preferred_element_type=jnp.float32
    )


def body(
    tokens,
    kept_index,
    kept_count,
    prompts,
    gain_one,
    shift_one,
    w_query,
    b_query,
    w_key,
    w_value,
    b_value,
    w_out,
    b_out,
    gain_two,
    shift_two,
    w_fc1,
    b_fc1,
    w_fc2,
    b_fc2,
    cotangent,
):
    own_images = tokens.shape[0]
    model_width = tokens.shape[2]
    seq_rows = cotangent.shape[1]
    prompt_count = prompts.shape[0]
    patch_count = kept_index.shape[1]
    local_width = w_query.shape[1]
    local_heads = local_width // HEAD_DIM
    row_count = own_images * seq_rows
    score_scale = HEAD_DIM ** (-0.5)
    stream_in = assemble(tokens, prompts, kept_index, kept_count, seq_rows)
    normed_one, pull_one = jax.vjp(
        layer_norm, stream_in, gain_one.astype(jnp.float32), shift_one.astype(jnp.float32)
    )
    group_normed, group_counts = (
        lax.all_gather(normed_one.astype(jnp.bfloat16), "head", axis=0, tiled=True),
        lax.all_gather(kept_count.astype(jnp.bfloat16), "head", axis=0, tiled=True),
    )
    group_images = group_normed.shape[0]
    flat_rows = group_normed.reshape(group_images * seq_rows, model_width)
    queries = (
        jnp.dot(flat_rows, w_query, preferred_element_type=jnp.float32)
        + b_query.astype(jnp.float32)
    ).astype(jnp.bfloat16)
    key_rows = jnp.dot(flat_rows, w_key, preferred_element_type=jnp.float32).astype(jnp.bfloat16)
    value_rows = (
        jnp.dot(flat_rows, w_value, preferred_element_type=jnp.float32)
        + b_value.astype(jnp.float32)
    ).astype(jnp.bfloat16)
    limit_rows = 1.0 + prompt_count + group_counts.astype(jnp.float32)
    key_live = jnp.arange(seq_rows, dtype=jnp.float32)[None, :] < limit_rows[:, None]
    per_block = math.gcd(group_images, max(1, 512 // seq_rows))
    block_count = group_images // per_block
    live_blocks = key_live.reshape(block_count, per_block, seq_rows)

    def split_blocks(array):
        return array.reshape(block_count, per_block, seq_rows, local_heads, HEAD_DIM)

    def block_scores(query_block, key_block, live_block):
        raw_scores = (
            jnp.einsum(
                "bqhe,bkhe->bhqk", query_block, key_block, preferred_element_type=jnp.float32
            )
            * score_scale
        )
        return jnp.where(live_block[:, None, None, :], raw_scores, -1e30)

    def attend(pieces):
        query_block, key_block, value_block, live_block = pieces
        scores = block_scores(query_block, key_block, live_block)
        row_max = jnp.max(scores, axis=-1, keepdims=True)
        weights = jnp.exp(scores - row_max)
        totals = jnp.sum(weights, axis=-1, keepdims=True)
        attn_probs = (weights / totals).astype(jnp.bfloat16)
        mixed_block = jnp.einsum(
            "bhqk,bkhe->bqhe", attn_probs, value_block, preferred_element_type=jnp.float32
        ).astype(jnp.bfloat16)
        return (mixed_block, (row_max + jnp.log(totals))[..., 0])

    mixed_blocks, log_totals = lax.map(
        attend,
        (split_blocks(queries), split_blocks(key_rows), split_blocks(value_rows), live_blocks),
    )
    mixed_flat = mixed_blocks.reshape(group_images * seq_rows, local_width)
    branch_sum = lax.psum_scatter(
        jnp.dot(mixed_flat, w_out, preferred_element_type=jnp.float32),
        "head",
        scatter_dimension=0,
        tiled=True,
    )
    branch = branch_sum + b_out.astype(jnp.float32)
    stream_mid = stream_in + branch.reshape(own_images, seq_rows, model_width)
    normed_two, pull_two = jax.vjp(
        layer_norm, stream_mid, gain_two.astype(jnp.float32), shift_two.astype(jnp.float32)
    )
    normed_low = normed_two.astype(jnp.bfloat16).reshape(row_count, model_width)
    fc1_full, fc2_full, bias_full = (
        lax.all_gather(w_fc1, ("batch", "head"), axis=0, tiled=True),
        lax.all_gather(w_fc2, ("batch", "head"), axis=0, tiled=True),
        lax.all_gather(b_fc1, ("batch", "head"), axis=0, tiled=True),
    )
    before = contract_cols(normed_low, fc1_full) + bias_full.astype(jnp.float32)
    hidden_full, gelu_pull = jax.vjp(partial(jax.nn.gelu, approximate=True), before)
    hidden = hidden_full.astype(jnp.bfloat16)
    result = jnp.dot(hidden, fc2_full, preferred_element_type=jnp.float32) + b_fc2.astype(
        jnp.float32
    )
    row_live = (
        jnp.arange(seq_rows, dtype=jnp.int32)[None, :] < (1 + prompt_count + kept_count)[:, None]
    )
    stream_out = jnp.where(
        row_live[:, :, None], stream_mid + result.reshape(own_images, seq_rows, model_width), 0.0
    )
    layer_out = stream_out.astype(jnp.bfloat16)
    grad_out = jnp.where(row_live[:, :, None], cotangent.astype(jnp.float32), 0.0).reshape(
        row_count, model_width
    )
    grad_low = grad_out.astype(jnp.bfloat16)
    fc1_back, fc2_back = (fc1_full, fc2_full)
    grad_fc2 = contract_rows(hidden, grad_low)
    grad_bias_two = jnp.sum(grad_out, axis=0)
    grad_hidden = contract_cols(grad_low, fc2_back)
    grad_before = gelu_pull(grad_hidden)[0].astype(jnp.bfloat16)
    grad_fc1 = contract_rows(grad_before, normed_low)
    grad_bias_fc1 = jnp.sum(grad_before.astype(jnp.float32), axis=0)
    grad_normed_two = jnp.dot(grad_before, fc1_back, preferred_element_type=jnp.float32)
    grad_mid_norm, grad_gain_two, grad_shift_two = pull_two(
        grad_normed_two.reshape(own_images, seq_rows, model_width)
    )
    grad_mid = grad_out.reshape(own_images, seq_rows, model_width) + grad_mid_norm
    part_fc1, part_fc2, part_bias_fc1 = (
        lax.psum_scatter(grad_fc1, ("batch", "head"), scatter_dimension=0, tiled=True),
        lax.psum_scatter(grad_fc2, ("batch", "head"), scatter_dimension=0, tiled=True),
        lax.psum_scatter(grad_bias_fc1, ("batch", "head"), scatter_dimension=0, tiled=True),
    )
    grad_branch = grad_mid.astype(jnp.bfloat16).reshape(row_count, model_width)
    grad_bias_out = jnp.sum(grad_branch.astype(jnp.float32), axis=0)
    group_grad = lax.all_gather(grad_branch, "head", axis=0, tiled=True)
    grad_w_out = contract_rows(mixed_flat, group_grad)
    grad_mixed = contract_cols(group_grad, w_out).astype(jnp.bfloat16)

    def attend_back(pieces):
        query_block, key_block, value_block, live_block, log_block, grad_block = pieces
        scores = block_scores(query_block, key_block, live_block)
        probs_full = jnp.exp(scores - log_block[..., None])
        probs_low = probs_full.astype(jnp.bfloat16)
        grad_value = jnp.einsum(
            "bhqk,bqhe->bkhe", probs_low, grad_block, preferred_element_type=jnp.float32
        )
        grad_probs = jnp.einsum(
            "bqhe,bkhe->bhqk", grad_block, value_block, preferred_element_type=jnp.float32
        )
        inner_sum = jnp.sum(grad_probs * probs_full, axis=-1, keepdims=True)
        grad_scores = (probs_full * (grad_probs - inner_sum)).astype(jnp.bfloat16)
        grad_query = (
            jnp.einsum(
                "bhqk,bkhe->bqhe", grad_scores, key_block, preferred_element_type=jnp.float32
            )
            * score_scale
        )
        grad_key = (
            jnp.einsum(
                "bhqk,bqhe->bkhe", grad_scores, query_block, preferred_element_type=jnp.float32
            )
            * score_scale
        )
        return (
            grad_query.astype(jnp.bfloat16),
            grad_key.astype(jnp.bfloat16),
            grad_value.astype(jnp.bfloat16),
        )

    grad_query_blocks, grad_key_blocks, grad_value_blocks = lax.map(
        attend_back,
        (
            split_blocks(queries),
            split_blocks(key_rows),
            split_blocks(value_rows),
            live_blocks,
            log_totals,
            split_blocks(grad_mixed),
        ),
    )
    grad_queries = grad_query_blocks.reshape(group_images * seq_rows, local_width)
    grad_keys = grad_key_blocks.reshape(group_images * seq_rows, local_width)
    grad_values = grad_value_blocks.reshape(group_images * seq_rows, local_width)
    grad_w_query = contract_rows(flat_rows, grad_queries)
    grad_w_key = contract_rows(flat_rows, grad_keys)
    grad_w_value = contract_rows(flat_rows, grad_values)
    grad_b_query = jnp.sum(grad_queries.astype(jnp.float32), axis=0)
    grad_b_value = jnp.sum(grad_values.astype(jnp.float32), axis=0)
    grad_normed_one = lax.psum_scatter(
        (
            contract_cols(grad_queries, w_query)
            + contract_cols(grad_keys, w_key)
            + contract_cols(grad_values, w_value)
        ).astype(jnp.bfloat16),
        "head",
        scatter_dimension=0,
        tiled=True,
    ).astype(jnp.float32)
    grad_in_norm, grad_gain_one, grad_shift_one = pull_one(
        grad_normed_one.reshape(own_images, seq_rows, model_width)
    )
    grad_in = grad_mid + grad_in_norm
    grad_leading = grad_in[:, 0:1, :]
    grad_prompts = jnp.sum(grad_in[:, 1 : 1 + prompt_count, :], axis=0)
    placer = selector(kept_index, kept_count, patch_count, 0).astype(jnp.float32)
    grad_slots = grad_in[:, 1 + prompt_count : 1 + prompt_count + patch_count, :]
    grad_patches = jnp.einsum(
        "bip,bid->bpd",
        placer,
        grad_slots,
        precision=lax.Precision.HIGHEST,
        preferred_element_type=jnp.float32,
    )
    grad_tokens = jnp.concatenate([grad_leading, grad_patches], axis=1)
    attn_sums = lax.psum(
        (grad_w_query, grad_b_query, grad_w_key, grad_w_value, grad_b_value, grad_w_out), "batch"
    )
    shared_sums = lax.psum(
        (
            grad_prompts,
            grad_gain_one,
            grad_shift_one,
            grad_bias_out,
            grad_gain_two,
            grad_shift_two,
            grad_bias_two,
        ),
        ("batch", "head"),
    )
    return (
        layer_out,
        grad_tokens,
        shared_sums[0],
        shared_sums[1],
        shared_sums[2],
        attn_sums[0],
        attn_sums[1],
        attn_sums[2],
        attn_sums[3],
        attn_sums[4],
        attn_sums[5],
        shared_sums[3],
        shared_sums[4],
        shared_sums[5],
        part_fc1,
        part_bias_fc1,
        part_fc2,
        shared_sums[6],
    )


def solution(mesh):
    placed = (
        P(("batch", "head"), None, None),
        P(("batch", "head"), None),
        P(("batch", "head")),
        P(),
        P(),
        P(),
        P(None, "head"),
        P("head"),
        P(None, "head"),
        P(None, "head"),
        P("head"),
        P("head", None),
        P(),
        P(),
        P(),
        P(("batch", "head"), None),
        P(("batch", "head")),
        P(("batch", "head"), None),
        P(),
        P(("batch", "head"), None, None),
    )
    return jax.shard_map(
        body,
        mesh=mesh,
        in_specs=placed,
        out_specs=(
            P(("batch", "head"), None, None),
            P(("batch", "head"), None, None),
            P(),
            P(),
            P(),
            P(None, "head"),
            P("head"),
            P(None, "head"),
            P(None, "head"),
            P("head"),
            P("head", None),
            P(),
            P(),
            P(),
            P(("batch", "head"), None),
            P(("batch", "head")),
            P(("batch", "head"), None),
            P(),
        ),
        check_vma=False,
    )
```

profile of v0, /device:TPU:0, one launch (start us, length us, event | category | flops | bytes accessed | tf_op | source)
XLA Modules:
  0.0 821.4 jit_solution(5066890579538325862)
XLA Ops:
  8.1 0.8 convert_element_type.155
  10.9 0.9 fusion.80
  12.6 1.2 fusion.51
  15.2 2.4 all_gather.18
  20.1 1.2 dynamic-slice.1
  22.2 2.5 all-reduce
  25.5 1.6 fusion.16
  27.1 0.9 copy.72
  28.1 1.1 squeeze.33
  29.2 0.8 fusion.81
  32.2 1.8 fusion.82
  35.5 42.3 %all-reduce.1 = bf16[3072]{0:T(1024)(128)(2,1)S(1)} all-reduce(bf16[3072]{0:T(1024)(128)(2,1)S(1)} %dynamic-update-slice.1), channel_id=1, replica_groups=mesh['batch'=16,'head'=2] {'batch','head'}, use_global_device_ids=true, to_apply=%add.1 | all-reduce | flops 3072 | bytes 12288
  77.9 1.4 fusion.79
  79.6 25.0 %all-gather.4.cloned.1.call-done = bf16[3072,768]{1,0:T(8,128)(2,1)} async-done(((bf16[96,768]{1,0:T(8,128)(2,1)}), bf16[3072,768]{1,0:T(8,128)(2,1)}) %all-gather.4.cloned.1.call-update) | async-done | bytes 4718608 | tf_op jit(solution)/shard_map/all_gather | solution.py:156
  104.7 5.5 convolution_add_fusion
  110.2 59.9 %all-gather.6.cloned.1.call-done = bf16[3072,768]{1,0:T(8,128)(2,1)} async-done(((bf16[96,768]{1,0:T(8,128)(2,1)}), bf16[3072,768]{1,0:T(8,128)(2,1)}) %all-gather.6.cloned.1.call-update) | async-done | bytes 4718608 | tf_op jit(solution)/shard_map/all_gather | solution.py:157
  170.0 6.3 convert_reduce_fusion
  176.4 1.5 multiply_reduce_fusion.1
  178.3 1.0 copy-done.4
  179.5 2.6 all-gather
  182.1 0.9 copy-done.16
  183.1 1.3 convolution_convert_fusion
  184.4 1.9 copy.80
  186.3 1.1 squeeze.36
  187.4 3.0 multiply_reduce_fusion
  197.5 1.5 add_convert_fusion
  199.1 1.6 fusion.85
  200.7 2.7 fusion.86
  203.4 1.6 fusion.87
  205.7 1.4 convert_reduce_fusion.1
  207.1 1.6 fusion.34
  208.7 1.8 fusion.38
  211.3 2.6 fusion.35
  214.0 6.6 fusion.76
  220.9 7.8 fusion.59
  229.5 42.5 %all-reduce.4 = (f32[384]{0:T(512)}, f32[384]{0:T(512)}) all-reduce(f32[384]{0:T(512)S(1)} %reduce_sum.229, f32[384]{0:T(512)S(1)} %reduce_sum.231), channel_id=1, replica_groups=mesh['batch'=16,'head'=2] {'batch'}, use_global_device_ids=true, to_apply=%region_20.21 | all-reduce | flops 768 | bytes 6144 | tf_op jit(solution)/shard_map/psum | solution.py:276
  272.0 6.0 fusion.30
  278.7 1.4 copy.92
  280.1 38.1 %all-reduce.3 = (f32[768]{0:T(1024)}, f32[768]{0:T(1024)}, f32[768]{0:T(1024)}, f32[768]{0:T(1024)}, f32[768]{0:T(1024)}, /*index=5*/f32[3072]{0:T(1024)S(1)}, f32[768]{0:T(1024)}) all-reduce(f32[768]{0:T(1024)S(1)} %get-tuple-element.125, f32[768]{0:T(1024)S(1)} %get-tuple-element.128, ...), channel_id=1, replica_groups=mesh['batch'=16,'head'=2] {'batch','head'}, use_global_device_ids=true, to_apply=%region_15.16 | all-reduce | flops 7680 | bytes 61440 | tf_op jit(solution)/shard_map/psum | solution.py:279
  318.8 15.3 %all-reduce.9.cloned.1.call-done = f32[50,768]{1,0:T(8,128)} async-done(((f32[50,768]{1,0:T(8,128)}), f32[50,768]{1,0:T(8,128)}) %all-reduce.9.cloned.1.call-update) | async-done | bytes 153616 | tf_op jit(solution)/shard_map/psum | solution.py:279
  334.1 189.5 %all-reduce.11.cloned.1.call-done = (f32[768,384]{1,0:T(8,128)}, f32[768,384]{1,0:T(8,128)}, f32[768,384]{1,0:T(8,128)}, f32[384,768]{1,0:T(8,128)}) async-done(((f32[768,384]{1,0:T(8,128)}, f32[768,384]{1,0:T(8,128)}, f32[768,384]{1,0:T(8,128)}, f32[384,768]{1,0:T(8,128)}), (f32[768,384]{1,0:T(8,128)}, f32[768,384]{1,0:T(8,128)}, f32[768,384]{1,0:T(8,128)}, ...) | async-done | bytes 4718608 | tf_op jit(solution)/shard_map/psum | solution.py:276
  523.6 142.2 %reduce-scatter.9.cloned.1.call-done = f32[96,768]{1,0:T(8,128)} async-done(((f32[3072,768]{1,0:T(8,128)}), f32[96,768]{1,0:T(8,128)}) %reduce-scatter.9.cloned.1.call-update) | async-done | bytes 294928 | tf_op jit(solution)/shard_map/reduce_scatter | solution.py:190
  665.8 141.0 %reduce-scatter.11.cloned.1.call-done = f32[96,768]{1,0:T(8,128)} async-done(((f32[3072,768]{1,0:T(8,128)}), f32[96,768]{1,0:T(8,128)}) %reduce-scatter.11.cloned.1.call-update) | async-done | bytes 294928 | tf_op jit(solution)/shard_map/reduce_scatter | solution.py:191
  806.8 1.6 copy.137
  808.4 2.5 copy.138
  810.9 1.0 copy.139
  811.9 1.0 copy.140
  812.9 1.0 copy.141
  (160 shorter events, 22.8 us)
Async XLA Ops:
  8.0 24.1 %copy-start = (bf16[384,768]{1,0:T(8,128)(2,1)S(1)}, bf16[384,768]{1,0:T(8,128)(2,1)}, u32[]{:S(2)}) copy-start(bf16[384,768]{1,0:T(8,128)(2,1)} %param.31) | copy-start | bytes 1769476
  8.0 69.9 %reduce-scatter.5.cloned.1.call-start = ((), (), s32[]{:S(2)}) async-start(), calls=%async_computation.4 | async-start | bytes 2359296 | tf_op jit(solution)/shard_map/reduce_scatter | solution.py:143
  8.1 9.6 %copy-start.25 = (bf16[768,384]{1,0:T(8,128)(2,1)S(1)}, bf16[768,384]{1,0:T(8,128)(2,1)}, u32[]{:S(2)}) copy-start(bf16[768,384]{1,0:T(8,128)(2,1)} %param.28) | copy-start | bytes 1769476
  10.9 3.2 copy-start.32
  14.1 5.2 copy-start.23
  14.4 0.6 copy-start.29
  15.0 2.7 copy-start.27
  18.6 10.6 %copy-start.5 = (bf16[2,256,6,64]{1,0,3,2:T(2,128)(2,1)}, bf16[2,256,6,64]{1,0,3,2:T(2,128)(2,1)S(1)}, u32[]{:S(2)}) copy-start(bf16[2,256,6,64]{1,0,3,2:T(2,128)(2,1)S(1)} %squeeze.35) | copy-start | bytes 1179652
  22.2 7.8 copy-start.7
  29.2 1.3 copy-start.18
  30.0 1.7 copy-start.2
  31.7 3.6 copy-start.34
  31.7 3.6 copy-start.39
  31.7 46.2 %copy-start.35 = (bf16[768]{0:T(1024)(128)(2,1)S(1)}, bf16[768]{0:T(1024)(128)(2,1)}, u32[]{:S(2)}) copy-start(bf16[768]{0:T(1024)(128)(2,1)} %param.34) | copy-start | bytes 4612
  31.7 46.2 %copy-start.36 = (bf16[768]{0:T(1024)(128)(2,1)S(1)}, bf16[768]{0:T(1024)(128)(2,1)}, u32[]{:S(2)}) copy-start(bf16[768]{0:T(1024)(128)(2,1)} %param.33) | copy-start | bytes 4612
  34.0 70.7 %all-gather.4.cloned.1.call-start = ((), (), s32[]{:S(2)}) async-start(), calls=%async_computation.5 | async-start | bytes 4866048 | tf_op jit(solution)/shard_map/all_gather | solution.py:156
  34.6 135.5 %all-gather.6.cloned.1.call-start = ((), (), s32[]{:S(2)}) async-start(), calls=%async_computation.6 | async-start | bytes 4866048 | tf_op jit(solution)/shard_map/all_gather | solution.py:157
  35.2 170.5 %reduce-scatter.7.cloned.1.call-start = ((), (), s32[]{:S(2)}) async-start(), calls=%async_computation.7 | async-start | bytes 1179648 | tf_op jit(solution)/shard_map/reduce_scatter | solution.py:250
  170.0 6.4 copy-start.38
  176.4 1.6 copy-start.17
  176.4 2.9 copy-start.14
  178.3 1.0 copy-start.4
  182.1 0.9 copy-start.16
  187.4 3.1 copy-start.10
  187.4 3.1 copy-start.3
  190.5 1.0 copy-start.6
  190.5 1.5 copy-start.8
  191.5 1.1 copy-start.11
  192.6 1.2 copy-start.24
  193.3 2.3 copy-start.26
  194.4 3.1 copy-start.22
  194.9 0.7 copy-start.9
  196.8 0.7 copy-start.12
  199.0 135.1 %all-reduce.9.cloned.1.call-start = ((), (), s32[]{:S(2)}) async-start(), calls=%async_computation.8 | async-start | bytes 344064 | tf_op jit(solution)/shard_map/psum | solution.py:279
  199.1 4.3 copy-start.13
  200.7 6.4 copy-start.30
  200.7 6.4 copy-start.28
  200.7 8.0 copy-start.15
  211.2 312.4 %all-reduce.11.cloned.1.call-start = ((), (), s32[]{:S(2)}) async-start(), calls=%async_computation.11 | async-start | bytes 9437184 | tf_op jit(solution)/shard_map/psum | solution.py:276
  213.9 451.8 %reduce-scatter.9.cloned.1.call-start = ((), (), s32[]{:S(2)}) async-start(), calls=%async_computation.9 | async-start | bytes 9732096 | tf_op jit(solution)/shard_map/reduce_scatter | solution.py:190
  220.6 586.2 %reduce-scatter.11.cloned.1.call-start = ((), (), s32[]{:S(2)}) async-start(), calls=%async_computation.10 | async-start | bytes 9732096 | tf_op jit(solution)/shard_map/reduce_scatter | solution.py:191
  228.7 0.7 copy-start.37
  272.0 6.0 copy-start.31
  272.0 6.1 copy-start.33
  523.6 287.3 %copy-start.21 = (f32[768,384]{1,0:T(8,128)S(1)}, f32[768,384]{1,0:T(8,128)}, u32[]{:S(2)}) copy-start(f32[768,384]{1,0:T(8,128)} %get-tuple-element.173) | copy-start | bytes 3538948
  523.6 288.3 %copy-start.20 = (f32[768,384]{1,0:T(8,128)S(1)}, f32[768,384]{1,0:T(8,128)}, u32[]{:S(2)}) copy-start(f32[768,384]{1,0:T(8,128)} %get-tuple-element.174) | copy-start | bytes 3538948
  808.4 4.5 copy-start.19
  808.4 5.5 copy-start.1
Sparse Core Ops, SparseCore 0:
  34.1 11.6 reduce-scatter.4
  199.1 6.4 reduce-scatter.6
Sparse Core Ops, SparseCore 1:
  37.8 66.8 all-gather.3
  107.9 62.1 all-gather.5
  211.3 122.8 all-reduce.8
  341.3 182.2 all-reduce.10
  531.1 134.6 reduce-scatter.8
  672.3 134.5 reduce-scatter.10
where the time goes:
time: 822 us; the launch traced here: 821 us
  waiting for transfers between devices  575 us (70%)
  blocking collectives  130 us (16%)
  matrix products  59.1 us (7%)
  local copies, waits for them, and re-layouts  25.4 us (3%)
  between operations  16.9 us (2%)
  other arithmetic  14.2 us (2%)
    psum x1, waiting for transfers between devices, body(): lax.psum((grad_w_query, grad_b_query, grad_w_key, grad_w_value, grad_b_va...  189 us
    reduce_scatter x1, waiting for transfers between devices, body(): lax.psum_scatter(grad_fc1, ('batch', 'head'), scatter_dimension=0, tiled=...  142 us
    reduce_scatter x1, waiting for transfers between devices, body(): lax.psum_scatter(grad_fc2, ('batch', 'head'), scatter_dimension=0, tiled=...  141 us
    all_gather x1, waiting for transfers between devices, body(): lax.all_gather(w_fc2, ('batch', 'head'), axis=0, tiled=True)  59.9 us
    unnamed x2, blocking collectives  44.8 us
    psum x1, blocking collectives, body(): lax.psum((grad_w_query, grad_b_query, grad_w_key, grad_w_value, grad_b_va...  42.5 us
    psum x1, blocking collectives, body(): lax.psum((grad_prompts, grad_gain_one, grad_shift_one, grad_bias_out, gra...  38.1 us
    all_gather x1, waiting for transfers between devices, body(): lax.all_gather(w_fc1, ('batch', 'head'), axis=0, tiled=True)  25 us
  transfers between devices with their start and end apart: 8, of which 7 were waited for; matrix products, arithmetic and copies ran while one was open for 5% of the time, Pallas kernels for 0%

commit v1 on v0

v1 whole, which is shorter than its diff:
```python
import functools
from types import SimpleNamespace

import jax
import jax.numpy as jnp
from jax import lax
from jax.experimental import pallas as pl
from jax.experimental.pallas import tpu as pltpu
from jax.sharding import PartitionSpec as P

MESH = pl.DeviceIdType.MESH
HEAD_DIM = 64
EPSILON = 1e-06
LANES = 128
BF16 = jnp.bfloat16
F32 = jnp.float32


def round_up(value, step):
    return -(-value // step) * step


def mm(left, right):
    return lax.dot_general(left, right, (((1,), (0,)), ((), ())), preferred_element_type=F32)


def mm_nt(left, right):
    return lax.dot_general(left, right, (((1,), (1,)), ((), ())), preferred_element_type=F32)


def mm_tn(left, right):
    return lax.dot_general(left, right, (((0,), (0,)), ((), ())), preferred_element_type=F32)


def fold_rows(rows):
    count, width = rows.shape
    return jnp.sum(rows.reshape(count // 8, 8, width), axis=0)


def normalise(rows):
    width = rows.shape[1]
    centre = jnp.sum(rows, axis=1, keepdims=True) * (1.0 / width)
    centred = rows - centre
    spread = jnp.sum(centred * centred, axis=1, keepdims=True) * (1.0 / width)
    scale = lax.rsqrt(spread + EPSILON)
    return centred * scale, scale


def norm_back(grad_rows, gain_row, unit_rows, scale):
    width = grad_rows.shape[1]
    scaled = grad_rows * gain_row
    mean_one = jnp.sum(scaled, axis=1, keepdims=True) * (1.0 / width)
    mean_two = jnp.sum(scaled * unit_rows, axis=1, keepdims=True) * (1.0 / width)
    return scale * (scaled - mean_one - unit_rows * mean_two)


GELU_A = 0.7978845608028654
GELU_B = 0.044715


def gelu_both(value):
    square = value * value
    bend = jnp.tanh(value * (GELU_A + (GELU_A * GELU_B) * square))
    half = 0.5 + 0.5 * bend
    slope = half + (0.5 * value) * (1.0 - bend * bend) * (
        GELU_A + (3.0 * GELU_A * GELU_B) * square
    )
    return value * half, slope


class Links:
    def __init__(self, send_sems, recv_sems):
        self.send_sems = send_sems
        self.recv_sems = recv_sems
        self.copies = []

    def send(self, source, target, device):
        place = len(self.copies)
        copy = pltpu.make_async_remote_copy(
            src_ref=source,
            dst_ref=target,
            send_sem=self.send_sems.at[place],
            recv_sem=self.recv_sems.at[place],
            device_id=device,
            device_id_type=MESH,
        )
        copy.start()
        self.copies.append(copy)
        return copy

    def drain(self):
        for copy in self.copies:
            copy.wait_send()


def layer_kernel(dims, *refs):
    it = iter(refs)
    tokens, kept, count_ref, prompts, vecs, wq, wk, wv, wout, fc1, fc2, cot = (
        next(it) for _ in range(12)
    )
    out_rows, out_tok, out_attn, out_small, out_fc1, out_fc2, out_bias = (
        next(it) for _ in range(7)
    )
    s = SimpleNamespace(**dict(zip(dims.scratch, it)))
    seq, width, local = dims.seq, dims.width, dims.local
    pairs = local // LANES
    rows_per = dims.rows_per
    n, ring, slots = dims.n, dims.ring, dims.slots
    chunk_slots = dims.chunk_slots
    chunk = chunk_slots * rows_per
    chunks = slots // chunk_slots
    tok_rows, tok_pad, prompt_pad = dims.tok_rows, dims.tok_pad, dims.prompt_pad
    prompt_rows, patches = dims.prompt_rows, dims.patches
    rest_count = n // 16
    score_scale = HEAD_DIM**-0.5
    block = 32
    blocks = seq // block

    b = lax.axis_index("batch")
    h = lax.axis_index("head")
    bx = b % 2
    by = (b // 2) % 2
    zz = b // 4
    sib = (b, 1 - h)
    xdev = (b + 1 - 2 * bx, h)
    ydev = (b + 2 - 4 * by, h)
    corner = b % 4
    ring_next = (((zz + 1) % ring) * 4 + corner, h)
    ring_prev = (((zz + ring - 1) % ring) * 4 + corner, h)
    zq = zz % 4
    zdev = [((zz - zq + (zq + hop) % 4) * 4 + corner, h) for hop in range(4)]
    rest = b // 16
    rdev = [(((rest + hop) % rest_count) * 16 + b % 16, h) for hop in range(rest_count)]
    one_dev = (xdev[0] * (1 - h) + ydev[0] * h, h)
    two_dev = (ydev[0] * (1 - h) + xdev[0] * h, h)
    p_one = bx * (1 - h) + by * h
    p_two = by * (1 - h) + bx * h

    partners = [sib, xdev, ydev] + zdev[1:]
    if ring > 4:
        partners += [ring_next, ring_prev] + rdev[1:]
    barrier = pltpu.get_barrier_semaphore()
    for partner in partners:
        pl.semaphore_signal(barrier, inc=1, device_id=partner, device_id_type=MESH)

    links = Links(s.send_sems, s.recv_sems)

    w_all, b_all, cot_all = s.w_all, s.b_all, s.cot_all
    w_all[0, 0:rows_per] = fc1[...]
    w_all[0, rows_per : 2 * rows_per] = fc2[...]
    b_all[0] = jnp.broadcast_to(vecs[7:8, 0:LANES], (8, LANES))
    limit = count_ref[0] + (1 + prompt_rows)
    s.meta[0] = jnp.broadcast_to(limit, (8, LANES))

    @pl.loop(0, blocks)
    def _(step):
        at = pl.ds(pl.multiple_of(step * block, block), block)
        row_ids = lax.broadcasted_iota(jnp.int32, (block, 1), 0) + step * block
        rows = cot[at, :].astype(F32)
        cot_all[0, at, :] = jnp.where(row_ids < limit, rows, 0.0).astype(BF16)

    pl.semaphore_wait(barrier, len(partners))

    gather_ring, gather_y = {}, {}

    def gather_step(distance):
        if distance > 0:
            for copy in gather_ring[distance]:
                copy.wait_recv()
        mine = 2 * distance
        if distance + 1 < ring:
            gather_ring[distance + 1] = [
                links.send(w_all.at[mine], w_all.at[mine + 2], ring_next),
                links.send(b_all.at[mine], b_all.at[mine + 2], ring_next),
            ]
        gather_y[distance] = [
            links.send(w_all.at[mine], w_all.at[mine + 1], ydev),
            links.send(b_all.at[mine], b_all.at[mine + 1], ydev),
        ]

    gather_done = [0]

    def gather_until(distance):
        while gather_done[0] <= min(distance, ring - 1):
            gather_step(gather_done[0])
            gather_done[0] += 1

    gather_until(0)
    cot_x = links.send(cot_all.at[0], cot_all.at[2], xdev)
    cot_sib = links.send(cot_all.at[0], cot_all.at[1], sib)
    meta_sib = links.send(s.meta.at[0], s.meta.at[1], sib)

    src, pick = s.src, s.pick
    src[...] = jnp.zeros(src.shape, BF16)
    src[0:tok_rows, :] = tokens[...]
    src[tok_pad : tok_pad + prompt_rows, :] = prompts[...]
    s.idx[...] = jnp.zeros((8, seq), jnp.int32)
    s.idx[0:1, 0:patches] = kept[...]
    shifted = pltpu.roll(s.idx[...], 1 + prompt_rows, axis=1)[0:1, :]
    spot = lax.broadcasted_iota(jnp.int32, (1, seq), 1)
    wanted = jnp.where(
        spot < 1 + prompt_rows,
        jnp.where(spot == 0, 0, tok_pad - 1 + spot),
        jnp.where(spot < limit, shifted + 1, -1),
    )
    pick[...] = jnp.where(
        lax.broadcasted_iota(jnp.int32, pick.shape, 0) == wanted, 1.0, 0.0
    ).astype(BF16)
    stream = s.stream
    stream[...] = mm_tn(pick[...], src[...])

    n1 = s.n1

    @pl.loop(0, blocks)
    def _(step):
        at = pl.ds(pl.multiple_of(step * block, block), block)
        unit_rows, _ = normalise(stream[at, :])
        n1[0, at, :] = (unit_rows * vecs[0:1, :] + vecs[1:2, :]).astype(BF16)

    n1_sib = links.send(n1.at[0], n1.at[1], sib)

    def project(image):
        rows = n1[image]
        queries = mm(rows, wq[...]) + vecs[6:7, 0:local]
        keys = mm(rows, wk[...])
        values = mm(rows, wv[...]) + vecs[6:7, local : 2 * local]
        for pair in range(pairs):
            at = slice(pair * LANES, (pair + 1) * LANES)
            s.q[image, pair] = queries[:, at].astype(BF16)
            s.k[image, pair] = keys[:, at].astype(BF16)
            s.v[image, pair] = values[:, at].astype(BF16)

    lane_ids = lax.broadcasted_iota(jnp.int32, (1, LANES), 1)
    lane_half = [
        jnp.where(lane_ids // HEAD_DIM == half, 1.0, 0.0).astype(BF16) for half in range(2)
    ]
    key_ids = lax.broadcasted_iota(jnp.int32, (seq, 1), 0)

    def attend(image):
        key_live = key_ids < s.meta[image, 0:1, 0:1]

        @pl.loop(0, pairs)
        def _(pair):
            queries, keys = s.q[image, pair], s.k[image, pair]
            values_t = s.v[image, pair].T
            for half in range(2):
                scores = mm_nt(keys, queries * lane_half[half]) * score_scale
                scores = jnp.where(key_live, scores, -1e30)
                weights = jnp.exp(scores - jnp.max(scores, axis=0, keepdims=True))
                probs = weights * (1.0 / jnp.sum(weights, axis=0, keepdims=True))
                s.probs[image * 2 * pairs + pair * 2 + half] = probs
                mixed_t = mm(values_t[half * HEAD_DIM : (half + 1) * HEAD_DIM], probs.astype(BF16))
                at = pl.ds(pl.multiple_of(pair * LANES + half * HEAD_DIM, HEAD_DIM), HEAD_DIM)
                s.mixed_t[image, at, :] = mixed_t.astype(BF16)

    project(0)
    n1_sib.wait_recv()
    meta_sib.wait_recv()
    project(1)
    attend(1)
    s.branch_out[...] = mm_tn(s.mixed_t[1], wout[...])
    branch_sib = links.send(s.branch_out, s.branch_in, sib)
    gather_until(1)
    attend(0)
    s.branch_own[...] = mm_tn(s.mixed_t[0], wout[...])
    branch_sib.wait_recv()

    middle, n2 = s.middle, s.n2

    @pl.loop(0, blocks)
    def _(step):
        at = pl.ds(pl.multiple_of(step * block, block), block)
        rows = stream[at, :] + (s.branch_own[at, :] + s.branch_in[at, :] + vecs[2:3, :])
        middle[at, :] = rows
        unit_rows, _ = normalise(rows)
        n2[0, at, :] = (unit_rows * vecs[3:4, :] + vecs[4:5, :]).astype(BF16)

    n2_x = links.send(n2.at[0], n2.at[2], xdev)
    n2_sib = links.send(n2.at[0], n2.at[1], sib)
    cot_x.wait_recv()
    cot_far = links.send(cot_all.at[2], cot_all.at[3], sib)
    gather_until(ring // 2)

    hidden_all, before_all = s.hidden, s.grad_before
    result, grad_two = s.result, s.grad_two
    unpack = jnp.where(
        lax.broadcasted_iota(jnp.int32, (LANES, chunk), 1) % rows_per
        == lax.broadcasted_iota(jnp.int32, (LANES, chunk), 0),
        1.0,
        0.0,
    )
    owner_of = (
        lax.broadcasted_iota(jnp.int32, (chunk_slots, chunk), 1) // rows_per
        == lax.broadcasted_iota(jnp.int32, (chunk_slots, chunk), 0)
    )

    def feed(part, images):
        first = part * chunk_slots
        span = slice(first, first + chunk_slots)
        tiles = b_all[span, 0, :].astype(BF16)
        bias_row = jnp.sum(
            jnp.where(owner_of, mm(tiles, unpack.astype(BF16)), 0.0), axis=0, keepdims=True
        )

        def one(image, total):
            up = w_all[span, 0:rows_per].reshape(chunk, width)
            down = w_all[span, rows_per : 2 * rows_per].reshape(chunk, width)
            before = mm_nt(n2[image], up) + bias_row
            hidden, slope = gelu_both(before)
            hidden = hidden.astype(BF16)
            hidden_all[image] = hidden
            grad_before = (mm_nt(cot_all[image], down) * slope).astype(BF16)
            before_all[image] = grad_before
            if part == 0:
                result[image] = mm(hidden, down)
                grad_two[image] = mm(grad_before, up)
            else:
                result[image] += mm(hidden, down)
                grad_two[image] += mm(grad_before, up)
            return total + fold_rows(grad_before.astype(F32))

        return lax.fori_loop(images[0], images[1], one, jnp.zeros((8, chunk), F32))

    g_all, gb_all = s.g_all, s.gb_all

    def feed_weights(part, bias_total):
        first = part * chunk_slots
        span = slice(first, first + chunk_slots)

        for left, right, base in ((before_all, n2, 0), (hidden_all, cot_all, rows_per)):
            total = jnp.zeros((chunk, width), F32)
            for image in range(4):
                total += mm_tn(left[image], right[image])
            g_all[span, base : base + rows_per] = (
                total.astype(BF16).reshape(chunk_slots, rows_per, width)
            )
        bias_row = jnp.sum(bias_total, axis=0, keepdims=True)
        spread = jnp.where(owner_of, jnp.broadcast_to(bias_row, owner_of.shape), 0.0)
        high = spread.astype(BF16)
        low = (spread - high.astype(F32)).astype(BF16)
        packed = mm_nt(high, unpack.astype(BF16)) + mm_nt(low, unpack.astype(BF16))
        for slot in range(chunk_slots):
            gb_all[first + slot] = jnp.broadcast_to(packed[slot : slot + 1], (8, LANES))

    order = list(range(1, ring)) + [0]
    sum_y, sum_ring = {}, {}

    def sum_send_y(distance):
        slot = 2 * distance + 1
        sum_y[distance] = [
            links.send(g_all.at[slot], s.ry.at[distance], ydev),
            links.send(gb_all.at[slot], s.ryb.at[distance], ydev),
        ]

    def sum_step(distance):
        for copy in sum_y[distance]:
            copy.wait_recv()
        mine = 2 * distance
        total = g_all[mine].astype(F32) + s.ry[distance].astype(F32)
        bias = gb_all[mine] + s.ryb[distance]
        if distance != 1:
            before = (distance + ring - 1) % ring
            for copy in sum_ring[before]:
                copy.wait_recv()
            total += s.rz_in[before].astype(F32)
            bias += s.rzb_in[before]
        if distance == 0:
            out_fc1[...] = total[0:rows_per]
            out_fc2[...] = total[rows_per : 2 * rows_per]
            out_bias[...] = bias
        else:
            s.rz_out[distance] = total.astype(BF16)
            s.rzb_out[distance] = bias
            sum_ring[distance] = [
                links.send(s.rz_out.at[distance], s.rz_in.at[distance], ring_next),
                links.send(s.rzb_out.at[distance], s.rzb_in.at[distance], ring_next),
            ]

    sums_done = [0]

    def sum_until(steps):
        while sums_done[0] < min(steps, ring):
            sum_step(order[sums_done[0]])
            sums_done[0] += 1

    def gather_wait(part):
        per = chunk_slots // 2
        gather_until((part + 1) * per)
        for distance in range(part * per, (part + 1) * per):
            for copy in gather_y[distance]:
                copy.wait_recv()

    gather_wait(0)
    n2_sib.wait_recv()
    cot_sib.wait_recv()
    near = feed(0, (0, 2))
    n2_x.wait_recv()
    n2_far = links.send(n2.at[2], n2.at[3], sib)
    gather_until(ring - 1)
    cot_far.wait_recv()
    n2_far.wait_recv()
    feed_weights(0, near + feed(0, (2, 4)))
    for distance in range(1, chunk_slots // 2):
        sum_send_y(distance)
    if chunks == 2:
        gather_wait(1)
        bias_total = feed(1, (0, 4))

    part_out, part_in = s.part_out, s.part_in
    cross_out, cross_in = s.cross_out, s.cross_in
    part_sib, cross = {}, {}
    for kind, total in enumerate((grad_two, result)):
        for place, image in enumerate((3, 1)):
            part_out[kind, place] = total[image].astype(BF16)
            part_sib[kind, place] = links.send(
                part_out.at[kind, place], part_in.at[kind, place], sib
            )
    for kind, total in enumerate((grad_two, result)):
        part_sib[kind, 0].wait_recv()
        cross_out[kind] = (total[2] + part_in[kind, 0].astype(F32)).astype(BF16)
        cross[kind] = links.send(cross_out.at[kind], cross_in.at[kind], xdev)
    if chunks == 2:
        feed_weights(1, bias_total)
    for distance in range(chunk_slots // 2, ring):
        sum_send_y(distance)
    sum_send_y(0)
    sum_until(1)

    part_sib[0, 1].wait_recv()
    cross[0].wait_recv()

    grad_mid, grad_branch = s.grad_mid, s.grad_branch

    def mid_back(step, totals):
        at = pl.ds(pl.multiple_of(step * block, block), block)
        grads = (
            grad_two[0, at, :] + part_in[0, 1, at, :].astype(F32) + cross_in[0, at, :].astype(F32)
        )
        unit_rows, scale = normalise(middle[at, :])
        passed = cot_all[0, at, :].astype(F32)
        mid = passed + norm_back(grads, vecs[3:4, :], unit_rows, scale)
        grad_mid[at, :] = mid
        low = mid.astype(BF16)
        grad_branch[0, at, :] = low
        return (
            totals[0] + fold_rows(grads * unit_rows),
            totals[1] + fold_rows(grads),
            totals[2] + fold_rows(low.astype(F32)),
            totals[3] + fold_rows(passed),
        )

    empty = jnp.zeros((8, width), F32)
    gain_two_sum, shift_two_sum, out_bias_sum, fc2_bias_sum = lax.fori_loop(
        0, blocks, mid_back, (empty,) * 4
    )
    branch_back = links.send(grad_branch.at[0], grad_branch.at[1], sib)

    def mixed_back(image):
        grads = mm_nt(grad_branch[image], wout[...])
        for pair in range(pairs):
            s.grad_mixed[image, pair] = grads[:, pair * LANES : (pair + 1) * LANES].astype(BF16)

    grads_qkv = s.grads_qkv

    def attend_back(image):
        @pl.loop(0, pairs)
        def _(pair):
            queries, keys = s.q[image, pair], s.k[image, pair]
            values, grads = s.v[image, pair], s.grad_mixed[image, pair]
            keys_t = keys.T
            grad_values = jnp.zeros((seq, LANES), F32)
            grad_keys = jnp.zeros((seq, LANES), F32)
            grad_queries = []
            for half in range(2):
                probs = s.probs[image * 2 * pairs + pair * 2 + half]
                grads_half = grads * lane_half[half]
                grad_values += mm(probs.astype(BF16), grads_half)
                grad_probs = mm_nt(values, grads_half)
                inner = jnp.sum(grad_probs * probs, axis=0, keepdims=True)
                grad_scores = (probs * (grad_probs - inner)).astype(BF16)
                grad_keys += mm(grad_scores, queries * lane_half[half])
                grad_queries.append(
                    mm(keys_t[half * HEAD_DIM : (half + 1) * HEAD_DIM], grad_scores)
                )
            grad_query = jnp.concatenate(grad_queries, axis=0).T
            for place, value in enumerate(
                (grad_query * score_scale, grad_keys * score_scale, grad_values)
            ):
                at = pl.ds(pl.multiple_of(place * local + pair * LANES, LANES), LANES)
                grads_qkv[image, :, at] = value.astype(BF16)

    def rows_back(image):
        return (
            mm_nt(grads_qkv[image, :, 0:local], wq[...])
            + mm_nt(grads_qkv[image, :, local : 2 * local], wk[...])
            + mm_nt(grads_qkv[image, :, 2 * local : 3 * local], wv[...])
        )

    mixed_back(0)
    branch_back.wait_recv()
    mixed_back(1)

    ar = s.ar
    flat = [
        (ar.at[item], s.ar_one.at[item], s.ar_two.at[item], s.ar_z.at[item],
         s.ar_rest.at[item], out_attn.at[item], width)
        for item in range(4)
    ]
    small_half = seq // 2
    small = (s.small, s.small_one, s.small_two, s.small_z, s.small_rest,
             s.small_all, small_half)
    items = flat + [small]
    stages = [dict() for _ in range(7)]

    def piece(total_rows):
        half, quarter, leaf = total_rows // 2, total_rows // 4, total_rows // 16
        at_one = pl.multiple_of(p_one * half, half)
        at_two = pl.multiple_of(at_one + p_two * quarter, quarter)
        return half, quarter, leaf, at_one, at_two

    def reduce_one(item):
        data, one = items[item][0], items[item][1]
        half, _, _, _, _ = piece(items[item][6])
        other = pl.ds(pl.multiple_of((1 - p_one) * half, half), half)
        stages[0][item] = [links.send(data.at[other], one, one_dev)]

    def reduce_two(item):
        data, one, two = items[item][:3]
        half, quarter, _, at_one, _ = piece(items[item][6])
        stages[0][item][0].wait_recv()
        mine = pl.ds(at_one, half)
        data[mine] = (data[mine].astype(F32) + one[...].astype(F32)).astype(data.dtype)
        other = pl.ds(pl.multiple_of(at_one + (1 - p_two) * quarter, quarter), quarter)
        stages[1][item] = [links.send(data.at[other], two, two_dev)]

    def reduce_z(item):
        data, _, two, by_z = items[item][:4]
        _, quarter, leaf, _, at_two = piece(items[item][6])
        stages[1][item][0].wait_recv()
        mine = pl.ds(at_two, quarter)
        data[mine] = (data[mine].astype(F32) + two[...].astype(F32)).astype(data.dtype)
        stages[2][item] = [
            links.send(
                data.at[pl.ds(pl.multiple_of(at_two + ((zq + hop) % 4) * leaf, leaf), leaf)],
                by_z.at[hop - 1],
                zdev[hop],
            )
            for hop in range(1, 4)
        ]

    def spread_z(item):
        data, _, _, by_z, by_rest, done = items[item][:6]
        _, _, leaf, _, at_two = piece(items[item][6])
        for copy in stages[2][item]:
            copy.wait_recv()
        mine = pl.ds(pl.multiple_of(at_two + zq * leaf, leaf), leaf)
        total = data[mine].astype(F32)
        for hop in range(3):
            total += by_z[hop].astype(F32)
        if rest_count > 1:
            by_rest[0] = total.astype(data.dtype)
            copies = [
                links.send(by_rest.at[0], by_rest.at[hop], rdev[hop])
                for hop in range(1, rest_count)
            ]
            for copy in copies:
                copy.wait_recv()
            total = jnp.zeros(total.shape, F32)
            for owner in range(rest_count):
                total += by_rest[(rest - owner + rest_count) % rest_count].astype(F32)
        done[mine] = total.astype(done.dtype)
        stages[3][item] = [
            links.send(done.at[mine], done.at[mine], zdev[hop]) for hop in range(1, 4)
        ]

    def spread_two(item):
        done = items[item][5]
        _, quarter, _, _, at_two = piece(items[item][6])
        for copy in stages[3][item]:
            copy.wait_recv()
        mine = pl.ds(at_two, quarter)
        stages[4][item] = [links.send(done.at[mine], done.at[mine], two_dev)]

    def spread_one(item):
        done = items[item][5]
        half, _, _, at_one, _ = piece(items[item][6])
        stages[4][item][0].wait_recv()
        mine = pl.ds(at_one, half)
        stages[5][item] = [links.send(done.at[mine], done.at[mine], one_dev)]

    def finish(item):
        stages[5][item][0].wait_recv()

    steps = [reduce_one, reduce_two, reduce_z, spread_z, spread_two, spread_one, finish]

    for half in range(2):
        at = slice(half * local, (half + 1) * local)
        total = mm(s.mixed_t[0], grad_branch[0, :, at]) + mm(
            s.mixed_t[1], grad_branch[1, :, at]
        )
        ar[0, at, :] = total.astype(BF16)
    reduce_one(0)
    attend_back(1)
    s.rows_out[...] = rows_back(1).astype(BF16)
    rows_sib = links.send(s.rows_out, s.rows_in, sib)
    sum_until(2)
    attend_back(0)
    s.rows_own[...] = rows_back(0)
    sum_until(3)

    for base in range(0, width, 256):
        rows = slice(base, base + 256)
        total = mm_tn(n1[0, :, rows], grads_qkv[0]) + mm_tn(n1[1, :, rows], grads_qkv[1])
        for place in range(3):
            ar[1 + place, rows, :] = total[:, place * local : (place + 1) * local].astype(BF16)
    for item in range(1, 4):
        reduce_one(item)
    reduce_two(0)
    sum_until(ring)

    part_sib[1, 1].wait_recv()
    cross[1].wait_recv()

    @pl.loop(0, blocks)
    def _(step):
        at = pl.ds(pl.multiple_of(step * block, block), block)
        row_ids = lax.broadcasted_iota(jnp.int32, (block, 1), 0) + step * block
        total = result[0, at, :] + part_in[1, 1, at, :].astype(F32) + cross_in[1, at, :].astype(F32)
        rows = middle[at, :] + (total + vecs[5:6, :])
        out_rows[at, :] = jnp.where(row_ids < limit, rows, 0.0).astype(BF16)

    rows_sib.wait_recv()

    def in_back(step, totals):
        at = pl.ds(pl.multiple_of(step * block, block), block)
        grads = (s.rows_own[at, :] + s.rows_in[at, :].astype(F32))
        unit_rows, scale = normalise(stream[at, :])
        grad_mid[at, :] += norm_back(grads, vecs[0:1, :], unit_rows, scale)
        return (totals[0] + fold_rows(grads * unit_rows), totals[1] + fold_rows(grads))

    gain_one_sum, shift_one_sum = lax.fori_loop(0, blocks, in_back, (empty,) * 2)
    grad_in = grad_mid[...]
    high = grad_in.astype(BF16)
    low = (grad_in - high.astype(F32)).astype(BF16)
    placed = mm(pick[...], high) + mm(pick[...], low)
    out_tok[...] = placed[0:tok_rows]

    small_ref, small_own = s.small_full, s.small
    small_ref[...] = jnp.zeros(small_ref.shape, F32)
    part_width = small_ref.shape[1]
    parts = width // part_width
    for part in range(parts):
        small_ref[part * prompt_pad : part * prompt_pad + prompt_pad, :] = placed[
            tok_pad : tok_pad + prompt_pad, part * part_width : (part + 1) * part_width
        ]
    base = parts * prompt_pad
    sums = (gain_one_sum, shift_one_sum, out_bias_sum, gain_two_sum, shift_two_sum, fc2_bias_sum)
    for place, total in enumerate(sums):
        row = jnp.sum(total, axis=0, keepdims=True)
        for part in range(parts):
            at = base + place * parts + part
            small_ref[at : at + 1, :] = row[:, part * part_width : (part + 1) * part_width]
    base += len(sums) * parts
    for place in range(2):
        at = slice(2 * place * local, 2 * place * local + local)
        row = jnp.sum(
            grads_qkv[0, :, at].astype(F32) + grads_qkv[1, :, at].astype(F32),
            axis=0,
            keepdims=True,
        )
        for head in range(2):
            chosen = row * (h if head == 1 else 1 - h).astype(F32)
            at = base + head * 4 + place * 2
            small_ref[at : at + 1, :] = chosen[:, 0:part_width]
            small_ref[at + 1 : at + 2, 0 : local - part_width] = chosen[:, part_width:local]
    theirs = pl.ds(pl.multiple_of((1 - h) * small_half, small_half), small_half)
    ours = pl.ds(pl.multiple_of(h * small_half, small_half), small_half)
    small_sib = links.send(small_ref.at[theirs], s.small_in, sib)
    small_sib.wait_recv()
    small_own[...] = small_ref[ours] + s.small_in[...]
    reduce_one(4)

    begun = [2, 1, 1, 1, 1]
    for wave in range(1, len(steps) + len(items)):
        for item in range(len(items)):
            stage = wave - item
            if begun[item] <= stage < len(steps):
                steps[stage](item)
                begun[item] = stage + 1
    out_small[ours] = s.small_all[...]
    small_back = links.send(out_small.at[ours], out_small.at[ours], sib)
    small_back.wait_recv()
    links.drain()


def layer(dims, operands):
    seq, width, local = dims.seq, dims.width, dims.local
    n, ring, slots, rows_per = dims.n, dims.ring, dims.slots, dims.rows_per
    pairs = local // LANES
    chunk = dims.chunk_slots * rows_per
    rest_count = n // 16
    small_half = seq // 2
    part_width = 256
    copies = 4 * ring + 4 * ring + 40 + 5 * (10 + rest_count)
    vmem = pltpu.VMEM
    shared = 2 * rows_per
    scratch = dict(
        send_sems=pltpu.SemaphoreType.DMA((copies,)),
        recv_sems=pltpu.SemaphoreType.DMA((copies,)),
        w_all=vmem((slots, shared, width), BF16),
        b_all=vmem((slots, 8, LANES), F32),
        cot_all=vmem((4, seq, width), BF16),
        meta=vmem((2, 8, LANES), jnp.int32),
        src=vmem((dims.tok_pad + dims.prompt_pad, width), BF16),
        pick=vmem((dims.tok_pad + dims.prompt_pad, seq), BF16),
        idx=vmem((8, seq), jnp.int32),
        stream=vmem((seq, width), F32),
        middle=vmem((seq, width), F32),
        n1=vmem((2, seq, width), BF16),
        n2=vmem((4, seq, width), BF16),
        q=vmem((2, pairs, seq, LANES), BF16),
        k=vmem((2, pairs, seq, LANES), BF16),
        v=vmem((2, pairs, seq, LANES), BF16),
        probs=vmem((4 * pairs, seq, seq), F32),
        mixed_t=vmem((2, local, seq), BF16),
        branch_out=vmem((seq, width), F32),
        branch_in=vmem((seq, width), F32),
        branch_own=vmem((seq, width), F32),
        hidden=vmem((4, seq, chunk), BF16),
        grad_before=vmem((4, seq, chunk), BF16),
        result=vmem((4, seq, width), F32),
        grad_two=vmem((4, seq, width), F32),
        part_out=vmem((2, 2, seq, width), BF16),
        part_in=vmem((2, 2, seq, width), BF16),
        cross_out=vmem((2, seq, width), BF16),
        cross_in=vmem((2, seq, width), BF16),
        g_all=vmem((slots, shared, width), BF16),
        gb_all=vmem((slots, 8, LANES), F32),
        ry=vmem((ring, shared, width), BF16),
        ryb=vmem((ring, 8, LANES), F32),
        rz_out=vmem((ring, shared, width), BF16),
        rzb_out=vmem((ring, 8, LANES), F32),
        rz_in=vmem((ring, shared, width), BF16),
        rzb_in=vmem((ring, 8, LANES), F32),
        grad_mid=vmem((seq, width), F32),
        grad_branch=vmem((2, seq, width), BF16),
        grad_mixed=vmem((2, pairs, seq, LANES), BF16),
        grads_qkv=vmem((2, seq, 3 * local), BF16),
        rows_out=vmem((seq, width), BF16),
        rows_in=vmem((seq, width), BF16),
        rows_own=vmem((seq, width), F32),
        ar=vmem((4, width, local), BF16),
        ar_one=vmem((4, width // 2, local), BF16),
        ar_two=vmem((4, width // 4, local), BF16),
        ar_z=vmem((4, 3, width // 16, local), BF16),
        ar_rest=vmem((4, rest_count, width // 16, local), BF16),
        small_full=vmem((seq, part_width), F32),
        small_in=vmem((small_half, part_width), F32),
        small=vmem((small_half, part_width), F32),
        small_one=vmem((small_half // 2, part_width), F32),
        small_two=vmem((small_half // 4, part_width), F32),
        small_z=vmem((3, small_half // 16, part_width), F32),
        small_rest=vmem((rest_count, small_half // 16, part_width), F32),
        small_all=vmem((small_half, part_width), F32),
    )
    dims = SimpleNamespace(**vars(dims), scratch=tuple(scratch))
    whole = pl.BlockSpec(memory_space=pltpu.VMEM)
    in_specs = [whole] * len(operands)
    in_specs[2] = pl.BlockSpec(memory_space=pltpu.SMEM)
    shape = jax.ShapeDtypeStruct
    return pl.pallas_call(
        functools.partial(layer_kernel, dims),
        out_shape=(
            shape((seq, width), BF16),
            shape((dims.tok_rows, width), F32),
            shape((4, width, local), BF16),
            shape((seq, part_width), F32),
            shape((rows_per, width), F32),
            shape((rows_per, width), F32),
            shape((8, LANES), F32),
        ),
        in_specs=in_specs,
        out_specs=[whole] * 7,
        scratch_shapes=list(scratch.values()),
        compiler_params=pltpu.CompilerParams(
            collective_id=0, has_side_effects=True, vmem_limit_bytes=60 * 2**20
        ),
    )(*operands)


def body(n, *arguments):
    (
        tokens, kept_index, kept_count, prompts, gain_one, shift_one, w_query, b_query, w_key,
        w_value, b_value, w_out, b_out, gain_two, shift_two, w_fc1, b_fc1, w_fc2, b_fc2, cotangent,
    ) = arguments
    seq, width = cotangent.shape[1:]
    local = w_query.shape[1]
    rows = w_fc1.shape[0]
    rows_per = round_up(rows, 16)
    ring = n // 4
    slots = 2 * ring
    halves = slots // 2
    chunk_slots = halves if (halves % 2 == 0 and halves * rows_per % LANES == 0) else slots
    tok_rows, prompt_rows = tokens.shape[1], prompts.shape[0]
    dims = SimpleNamespace(
        n=n, ring=ring, slots=slots, chunk_slots=chunk_slots, rows_per=rows_per, seq=seq,
        width=width, local=local, tok_rows=tok_rows, tok_pad=round_up(tok_rows, 16),
        prompt_rows=prompt_rows, prompt_pad=round_up(prompt_rows, 16),
        patches=kept_index.shape[1],
    )
    if rows_per != rows:
        spare = ((0, rows_per - rows), (0, 0))
        w_fc1, w_fc2 = jnp.pad(w_fc1, spare), jnp.pad(w_fc2, spare)
    vecs = jnp.stack(
        [
            gain_one, shift_one, b_out, gain_two, shift_two, b_fc2,
            jnp.concatenate([b_query, b_value]), jnp.pad(b_fc1, (0, width - rows)),
        ]
    ).astype(F32)
    operands = (
        tokens[0], kept_index, kept_count, prompts, vecs, w_query, w_key, w_value, w_out,
        w_fc1, w_fc2, cotangent[0],
    )
    out_rows, out_tok, out_attn, small, grad_fc1, grad_fc2, grad_bias = layer(dims, operands)
    prompt_pad = dims.prompt_pad
    part_width = small.shape[1]
    parts = width // part_width
    grad_prompts = jnp.concatenate(
        [small[part * prompt_pad : part * prompt_pad + prompt_rows] for part in range(parts)], axis=1
    )
    base = parts * prompt_pad
    vectors = small[base : base + 6 * parts].reshape(6, width)
    base += 6 * parts
    own = lax.dynamic_slice_in_dim(small, base + 4 * lax.axis_index("head"), 4, 0)
    own = own.reshape(2, 2 * part_width)[:, :local]
    grads = out_attn.astype(F32)
    grad_out = jnp.concatenate([grads[0, :local], grads[0, local:]], axis=1)
    return (
        out_rows[None], out_tok[None], grad_prompts, vectors[0], vectors[1], grads[1], own[0],
        grads[2], grads[3], own[1], grad_out, vectors[2], vectors[3], vectors[4],
        grad_fc1[:rows], grad_bias[0, :rows], grad_fc2[:rows], vectors[5],
    )


def solution(mesh):
    batch, head = mesh.axis_names
    both = (batch, head)
    placed = (
        P(both, None, None), P(both, None), P(both), P(), P(), P(), P(None, head), P(head),
        P(None, head), P(None, head), P(head), P(head, None), P(), P(), P(),
        P(both, None), P(both), P(both, None), P(), P(both, None, None),
    )
    return jax.shard_map(
        functools.partial(body, mesh.shape[batch]),
        mesh=mesh,
        in_specs=placed,
        out_specs=(
            P(both, None, None), P(both, None, None), P(), P(), P(), P(None, head), P(head),
            P(None, head), P(None, head), P(head), P(head, None), P(), P(), P(),
            P(both, None), P(both), P(both, None), P(),
        ),
        check_vma=False,
    )
```

time: 822 us -> 160 us (0.19)
  waiting for transfers between devices: 575 us -> 0 us
  Pallas kernels: 0 us -> 136 us
  blocking collectives: 130 us -> 0 us
  matrix products: 59.1 us -> 0 us
  between operations: 16.9 us -> 1.36 us
  other arithmetic: 14.2 us -> 5.06 us
  local copies, waits for them, and re-layouts: 25.4 us -> 17 us
    reduce_scatter x4 -> x0, waiting for transfers between devices: 284 us -> none  [the longest x1 142 us: body(): lax.psum_scatter(grad_fc1, ('batch', 'head'), scatter_dimension=0, tiled=...]
    psum x2 -> x0, waiting for transfers between devices: 205 us -> none  [the longest x1 189 us: body(): lax.psum((grad_w_query, grad_b_query, grad_w_key, grad_w_value, grad_b_va...]
    pallas_call x0 -> x1, Pallas kernels: none -> 136 us  [layer(): pl.pallas_call(functools.partial(layer_kernel, dims), out_shape=(shape((s...]
    all_gather x2 -> x0, waiting for transfers between devices: 84.9 us -> none  [the longest x1 59.9 us: body(): lax.all_gather(w_fc2, ('batch', 'head'), axis=0, tiled=True)]
    psum x2 -> x0, blocking collectives: 80.6 us -> none  [the longest x1 42.5 us: body(): lax.psum((grad_w_query, grad_b_query, grad_w_key, grad_w_value, grad_b_va...]
    dot_general x26 -> x0, matrix products: 59.1 us -> none  [the longest x6 22.9 us: contract_rows(): lax.dot_general(left, right, (((0,), (0,)), ((), ())), preferred_element_...]
    unnamed x2 -> x0, blocking collectives: 44.8 us -> none
    unnamed x96 -> x12, local copies, waits for them, and re-layouts: 17.2 us -> 4.75 us
  transfers between devices with their start and end apart: 8 -> 0, of which waited for: 7 -> 0; matrix products, arithmetic and copies ran while one was open for 5% -> 0% of each run, Pallas kernels for 0% -> 0%
where the time goes in v1:
time: 160 us; the launch traced here: 159 us
  Pallas kernels  136 us (85%)
  local copies, waits for them, and re-layouts  17 us (11%)
  other arithmetic  5.06 us (3%)
    pallas_call x1, Pallas kernels, layer(): pl.pallas_call(functools.partial(layer_kernel, dims), out_shape=(shape((s...  136 us
    unnamed x12, local copies, waits for them, and re-layouts  4.75 us
    another operation x9, local copies, waits for them, and re-layouts, body(): jnp.stack([gain_one, shift_one, b_out, gain_two, shift_two, b_fc2, jnp.co...  4.17 us

profile of v1, /device:TPU:0, one launch (start us, length us, event | category | flops | bytes accessed | tf_op | source)
XLA Modules:
  0.0 159.3 jit_solution(10676370111183165040)
XLA Ops:
  1.3 0.7 pad_maximum_fusion.2
  2.0 0.7 pad.4
  2.7 0.7 stack.27
  3.4 0.7 stack.28
  4.1 0.7 stack.29
  4.7 0.7 stack.30
  5.4 0.7 stack.31
  6.1 0.7 stack.32
  6.8 0.6 convert_element_type.8.refs_4_
  7.5 135.9 %shard_map.331 = (bf16[256,768]{1,0:T(8,128)(2,1)}, f32[197,768]{1,0:T(8,128)}, bf16[4,768,384]{2,1,0:T(8,128)(2,1)}, f32[256,256]{1,0:T(8,128)}, f32[96,768]{1,...) custom-call(bf16[197,768]{1,0:T(8,128)(2,1)} %bitcast.19, s32[1,196]{1,0:T(1,128)} %refs_1_.1, s32[1]{0:T(128)S(6)} %copy.42.refs_2_, ...), custom_call_target="tpu_custom_call" | custom-call | tf_op jit(solution)/shard_map/pallas_call | solution.py:771
  143.3 0.0 copy-start.3
  143.4 2.6 %copy.38 = f32[1,197,768]{2,0,1:T(1,128)} copy(f32[1,197,768]{2,1,0:T(8,128)} %bitcast.16) | data formatting | bytes 1210368
  145.9 1.2 slice_bitcast_fusion.5
  147.1 0.0 copy-done.3
  147.1 0.6 slice_reduce_fusion
  147.8 0.7 pad_maximum_fusion.1
  148.4 0.6 squeeze.63
  149.0 0.6 squeeze.61
  149.6 0.6 squeeze.60
  150.2 0.6 squeeze.59
  150.8 0.6 squeeze.51
  151.4 0.6 squeeze.50
  152.0 2.0 %convert_element_type.9 = f32[4,768,384]{2,1,0:T(8,128)S(1)} convert(bf16[4,768,384]{2,1,0:T(8,128)(2,1)} %get-tuple-element.28) | non-fusion elementwise | flops 1179648 | bytes 7077888 | tf_op jit(solution)/shard_map/convert_element_type | solution.py:836
  154.0 0.1 slice_bitcast_fusion.4
  154.1 1.9 %slice_bitcast_fusion = (f32[768,384]{1,0:T(8,128)}, f32[768,384]{1,0:T(8,128)}, f32[768,384]{1,0:T(8,128)}) fusion(f32[4,768,384]{2,1,0:T(8,128)S(1)} %convert_element_type.9), kind=kLoop, calls=%fused_computation | loop fusion | bytes 7077888 | tf_op jit(solution)/shard_map/squeeze | solution.py:840
  156.0 0.0 copy-start
  156.0 0.0 copy-start.2
  156.0 1.1 pad_maximum_fusion
  157.1 0.0 copy-done
  157.1 0.0 copy-start.1
  157.1 0.7 copy.43
  157.8 0.0 copy-done.2
  157.8 0.7 copy.44
  158.5 0.0 copy-done.1
  158.5 0.7 copy.45
  (7 shorter events, 0.1 us)
Async XLA Ops:
  143.3 3.8 %copy-start.3 = (f32[256,256]{1,0:T(8,128)S(1)}, f32[256,256]{1,0:T(8,128)}, u32[]{:S(2)}) copy-start(f32[256,256]{1,0:T(8,128)} %get-tuple-element.27) | copy-start | bytes 786436
  156.0 1.1 copy-start
  156.0 1.9 %copy-start.2 = (f32[96,768]{1,0:T(8,128)S(1)}, f32[96,768]{1,0:T(8,128)}, u32[]{:S(2)}) copy-start(f32[96,768]{1,0:T(8,128)} %get-tuple-element.98) | copy-start | bytes 884740
  157.1 1.5 copy-start.1

commit v2 on v1

v2 whole, which is shorter than its diff:
```python
import functools
from types import SimpleNamespace

import jax
import jax.numpy as jnp
from jax import lax
from jax.experimental import pallas as pl
from jax.experimental.pallas import tpu as pltpu
from jax.sharding import PartitionSpec as P

MESH = pl.DeviceIdType.MESH
HEAD_DIM = 64
EPSILON = 1e-06
LANES = 128
BF16 = jnp.bfloat16
F32 = jnp.float32


def round_up(value, step):
    return -(-value // step) * step


def mm(left, right):
    return lax.dot_general(left, right, (((1,), (0,)), ((), ())), preferred_element_type=F32)


def mm_nt(left, right):
    return lax.dot_general(left, right, (((1,), (1,)), ((), ())), preferred_element_type=F32)


def mm_tn(left, right):
    return lax.dot_general(left, right, (((0,), (0,)), ((), ())), preferred_element_type=F32)


def fold_rows(rows):
    count, width = rows.shape
    return jnp.sum(rows.reshape(count // 8, 8, width), axis=0)


def normalise(rows):
    width = rows.shape[1]
    centre = jnp.sum(rows, axis=1, keepdims=True) * (1.0 / width)
    centred = rows - centre
    spread = jnp.sum(centred * centred, axis=1, keepdims=True) * (1.0 / width)
    scale = lax.rsqrt(spread + EPSILON)
    return centred * scale, scale


def norm_back(grad_rows, gain_row, unit_rows, scale):
    width = grad_rows.shape[1]
    scaled = grad_rows * gain_row
    mean_one = jnp.sum(scaled, axis=1, keepdims=True) * (1.0 / width)
    mean_two = jnp.sum(scaled * unit_rows, axis=1, keepdims=True) * (1.0 / width)
    return scale * (scaled - mean_one - unit_rows * mean_two)


GELU_A = 0.7978845608028654
GELU_B = 0.044715


def gelu_both(value):
    square = value * value
    bend = jnp.tanh(value * (GELU_A + (GELU_A * GELU_B) * square))
    half = 0.5 + 0.5 * bend
    slope = half + (0.5 * value) * (1.0 - bend * bend) * (
        GELU_A + (3.0 * GELU_A * GELU_B) * square
    )
    return value * half, slope


VECTORS = (
    "gain_one", "shift_one", "b_query", "b_value", "b_out", "gain_two", "shift_two", "b_fc1", "b_fc2",
)


class Loads:
    def __init__(self, sems):
        self.sems = sems
        self.count = 0

    def start(self, source, target):
        copy = pltpu.make_async_copy(source, target, self.sems.at[self.count])
        copy.start()
        self.count += 1
        return copy


class Links:
    def __init__(self, send_sems, recv_sems):
        self.send_sems = send_sems
        self.recv_sems = recv_sems
        self.copies = []

    def send(self, source, target, device):
        place = len(self.copies)
        copy = pltpu.make_async_remote_copy(
            src_ref=source,
            dst_ref=target,
            send_sem=self.send_sems.at[place],
            recv_sem=self.recv_sems.at[place],
            device_id=device,
            device_id_type=MESH,
        )
        copy.start()
        self.copies.append(copy)
        return copy

    def drain(self):
        for copy in self.copies:
            copy.wait_send()


def layer_kernel(dims, *refs):
    it = iter(refs)
    count_ref = next(it)
    tokens, kept, prompts, fc1, fc2, cot = (next(it) for _ in range(6))
    weights_in = [next(it) for _ in range(4)]
    vectors_in = [next(it) for _ in range(9)]
    out_rows, out_tok, out_attn, out_small, out_fc1, out_fc2, out_bias = (
        next(it) for _ in range(7)
    )
    s = SimpleNamespace(**dict(zip(dims.scratch, it)))
    w_pair, wout = s.w_pair, s.wout
    vecs = s.vecs
    seq, width, local = dims.seq, dims.width, dims.local
    pairs = local // LANES
    rows_per = dims.rows_per
    n, ring, slots = dims.n, dims.ring, dims.slots
    chunk_slots = dims.chunk_slots
    chunk = chunk_slots * rows_per
    chunks = slots // chunk_slots
    tok_rows, tok_pad, prompt_pad = dims.tok_rows, dims.tok_pad, dims.prompt_pad
    prompt_rows, patches = dims.prompt_rows, dims.patches
    rest_count = n // 16
    score_scale = HEAD_DIM**-0.5
    block = 32
    blocks = seq // block

    b = lax.axis_index("batch")
    h = lax.axis_index("head")
    bx = b % 2
    by = (b // 2) % 2
    zz = b // 4
    sib = (b, 1 - h)
    xdev = (b + 1 - 2 * bx, h)
    ydev = (b + 2 - 4 * by, h)
    corner = b % 4
    ring_next = (((zz + 1) % ring) * 4 + corner, h)
    ring_prev = (((zz + ring - 1) % ring) * 4 + corner, h)
    zq = zz % 4
    zdev = [((zz - zq + (zq + hop) % 4) * 4 + corner, h) for hop in range(4)]
    rest = b // 16
    rdev = [(((rest + hop) % rest_count) * 16 + b % 16, h) for hop in range(rest_count)]
    one_dev = (xdev[0] * (1 - h) + ydev[0] * h, h)
    two_dev = (ydev[0] * (1 - h) + xdev[0] * h, h)
    p_one = bx * (1 - h) + by * h
    p_two = by * (1 - h) + bx * h

    partners = [sib, xdev, ydev] + zdev[1:]
    if ring > 4:
        partners += [ring_next, ring_prev] + rdev[1:]
    barrier = pltpu.get_barrier_semaphore()
    for partner in partners:
        pl.semaphore_signal(barrier, inc=1, device_id=partner, device_id_type=MESH)

    links = Links(s.send_sems, s.recv_sems)

    w_all, b_all, cot_all = s.w_all, s.b_all, s.cot_all
    loads = Loads(s.load_sems)
    load_kept = loads.start(kept, s.kept)
    load_fc = [
        loads.start(fc1, w_all.at[0, pl.ds(0, rows_per)]),
        loads.start(fc2, w_all.at[0, pl.ds(rows_per, rows_per)]),
    ]
    load_cot = loads.start(cot.at[0], cot_all.at[0])
    load_rows = [loads.start(tokens, s.tokens), loads.start(prompts, s.prompts)]
    load_vectors = [loads.start(ref, getattr(s, name)) for ref, name in zip(vectors_in, VECTORS)]
    load_weights = [loads.start(weights_in[3], wout)]
    for pair in range(pairs):
        for place in range(3):
            load_weights.append(
                loads.start(
                    weights_in[place].at[:, pl.ds(pair * LANES, LANES)],
                    w_pair.at[pair, :, pl.ds(place * LANES, LANES)],
                )
            )

    limit = count_ref[0] + (1 + prompt_rows)
    src, pick = s.src, s.pick
    s.meta[0] = jnp.broadcast_to(limit, (8, LANES))
    s.idx[...] = jnp.zeros((8, seq), jnp.int32)
    src[tok_rows - tok_rows % 16 : tok_pad] = jnp.zeros((tok_pad - tok_rows + tok_rows % 16, width), BF16)
    src[tok_pad:] = jnp.zeros((prompt_pad, width), BF16)
    vecs[...] = jnp.zeros(vecs.shape, F32)
    load_kept.wait()
    s.idx[0:1, 0:patches] = s.kept[...]
    shifted = pltpu.roll(s.idx[...], 1 + prompt_rows, axis=1)[0:1, :]
    spot = lax.broadcasted_iota(jnp.int32, (1, seq), 1)
    wanted = jnp.where(
        spot < 1 + prompt_rows,
        jnp.where(spot == 0, 0, tok_pad - 1 + spot),
        jnp.where(spot < limit, shifted + 1, -1),
    )
    pick[...] = jnp.where(
        lax.broadcasted_iota(jnp.int32, pick.shape, 0) == wanted, 1.0, 0.0
    ).astype(BF16)
    for copy in load_vectors:
        copy.wait()
    for place, name in enumerate(("gain_one", "shift_one", "b_out", "gain_two", "shift_two", "b_fc2")):
        vecs[place : place + 1, :] = getattr(s, name)[...].astype(F32).reshape(1, width)
    vecs[6:7, 0:local] = s.b_query[...].astype(F32).reshape(1, local)
    vecs[6:7, local : 2 * local] = s.b_value[...].astype(F32).reshape(1, local)
    bias_rows = s.b_fc1.shape[0]
    vecs[7:8, 0:bias_rows] = s.b_fc1[...].astype(F32).reshape(1, bias_rows)
    b_all[0] = jnp.broadcast_to(vecs[7:8, 0:LANES], (8, LANES))
    load_cot.wait()

    @pl.loop(0, blocks)
    def _(step):
        at = pl.ds(pl.multiple_of(step * block, block), block)
        row_ids = lax.broadcasted_iota(jnp.int32, (block, 1), 0) + step * block
        rows = cot_all[0, at, :].astype(F32)
        cot_all[0, at, :] = jnp.where(row_ids < limit, rows, 0.0).astype(BF16)

    for copy in load_rows:
        copy.wait()
    src[0:tok_rows, :] = s.tokens[0]
    src[tok_pad : tok_pad + prompt_rows, :] = s.prompts[...]
    stream = s.stream
    stream[...] = mm_tn(pick[...], src[...])

    n1 = s.n1

    @pl.loop(0, blocks)
    def _(step):
        at = pl.ds(pl.multiple_of(step * block, block), block)
        unit_rows, s.scale_one[at, :] = normalise(stream[at, :])
        s.unit_one[at, :] = unit_rows
        n1[0, at, :] = (unit_rows * vecs[0:1, :] + vecs[1:2, :]).astype(BF16)

    for copy in load_fc:
        copy.wait()
    pl.semaphore_wait(barrier, len(partners))

    gather_ring, gather_y = {}, {}

    def gather_step(distance, kind):
        if distance > 0:
            for copy in gather_ring[distance, kind]:
                copy.wait_recv()
        rows = pl.ds(kind * rows_per, rows_per)
        mine = 2 * distance

        def hand_on(slot, device):
            copies = [links.send(w_all.at[mine, rows], w_all.at[slot, rows], device)]
            if kind == 0:
                copies.append(links.send(b_all.at[mine], b_all.at[slot], device))
            return copies

        if distance + 1 < ring:
            gather_ring[distance + 1, kind] = hand_on(mine + 2, ring_next)
        gather_y[distance, kind] = hand_on(mine + 1, ydev)

    gather_done = [0]

    def gather_until(distance, kind):
        while gather_done[0] <= min(2 * distance + kind, 2 * ring - 1):
            gather_step(gather_done[0] // 2, gather_done[0] % 2)
            gather_done[0] += 1

    n1_sib = links.send(n1.at[0], n1.at[1], sib)
    gather_until(0, 1)
    cot_x = links.send(cot_all.at[0], cot_all.at[2], xdev)
    cot_sib = links.send(cot_all.at[0], cot_all.at[1], sib)
    meta_sib = links.send(s.meta.at[0], s.meta.at[1], sib)


    def project(image):
        rows = n1[image]
        for pair in range(pairs):
            found = mm(rows, w_pair[pair])
            at = slice(pair * LANES, (pair + 1) * LANES)
            s.q[image, pair] = (found[:, 0:LANES] + vecs[6:7, at]).astype(BF16)
            s.k[image, pair] = found[:, LANES : 2 * LANES].astype(BF16)
            at = slice(local + pair * LANES, local + (pair + 1) * LANES)
            s.v[image, pair] = (found[:, 2 * LANES :] + vecs[6:7, at]).astype(BF16)

    lane_ids = lax.broadcasted_iota(jnp.int32, (1, LANES), 1)
    lane_half = [
        jnp.where(lane_ids // HEAD_DIM == half, 1.0, 0.0).astype(BF16) for half in range(2)
    ]
    lane_scaled = [
        jnp.where(lane_ids // HEAD_DIM == half, score_scale, 0.0).astype(BF16) for half in range(2)
    ]
    lane_spare = [
        jnp.where(lane_ids == (1 - half) * HEAD_DIM, 1.0, 0.0).astype(BF16) for half in range(2)
    ]
    key_ids = lax.broadcasted_iota(jnp.int32, (seq, 1), 0)

    def attend(image, first, last):
        key_bias = jnp.where(key_ids < s.meta[image, 0:1, 0:1], 0.0, -1e30).astype(BF16)

        @pl.loop(first, last)
        def _(pair):
            queries, keys = s.q[image, pair], s.k[image, pair]
            values_t = s.v[image, pair].T
            for half in range(2):
                scores = mm_nt(
                    keys * lane_half[half] + key_bias * lane_spare[half],
                    queries * lane_scaled[half] + lane_spare[half],
                )
                weights = jnp.exp(scores - jnp.max(scores, axis=0, keepdims=True))
                probs = weights * (1.0 / jnp.sum(weights, axis=0, keepdims=True))
                s.probs[image * 2 * pairs + pair * 2 + half] = probs
                mixed_t = mm(values_t[half * HEAD_DIM : (half + 1) * HEAD_DIM], probs.astype(BF16))
                at = pl.ds(pl.multiple_of(pair * LANES + half * HEAD_DIM, HEAD_DIM), HEAD_DIM)
                s.mixed_t[image, at, :] = mixed_t.astype(BF16)

    for copy in load_weights:
        copy.wait()
    project(0)
    n1_sib.wait_recv()
    meta_sib.wait_recv()
    project(1)
    attend(1, 0, pairs)
    s.branch_out[...] = mm_tn(s.mixed_t[1], wout[...])
    branch_sib = links.send(s.branch_out, s.branch_in, sib)
    gather_until(1, 0)
    attend(0, 0, pairs)
    gather_until(1, 1)
    s.branch_own[...] = mm_tn(s.mixed_t[0], wout[...])
    branch_sib.wait_recv()
    middle, n2 = s.middle, s.n2

    @pl.loop(0, blocks)
    def _(step):
        at = pl.ds(pl.multiple_of(step * block, block), block)
        rows = stream[at, :] + (s.branch_own[at, :] + s.branch_in[at, :] + vecs[2:3, :])
        middle[at, :] = rows
        unit_rows, s.scale_two[at, :] = normalise(rows)
        s.unit_two[at, :] = unit_rows
        n2[0, at, :] = (unit_rows * vecs[3:4, :] + vecs[4:5, :]).astype(BF16)

    n2_x = links.send(n2.at[0], n2.at[2], xdev)
    n2_sib = links.send(n2.at[0], n2.at[1], sib)
    gather_until(2, 0)
    cot_x.wait_recv()
    cot_far = links.send(cot_all.at[2], cot_all.at[3], sib)
    hidden_all, before_all = s.hidden, s.grad_before
    result, grad_two = s.result, s.grad_two
    unpack = jnp.where(
        lax.broadcasted_iota(jnp.int32, (LANES, chunk), 1) % rows_per
        == lax.broadcasted_iota(jnp.int32, (LANES, chunk), 0),
        1.0,
        0.0,
    )
    owner_of = (
        lax.broadcasted_iota(jnp.int32, (chunk_slots, chunk), 1) // rows_per
        == lax.broadcasted_iota(jnp.int32, (chunk_slots, chunk), 0)
    )

    def feed_spans(part):
        span = slice(part * chunk_slots, (part + 1) * chunk_slots)
        return (
            w_all[span, 0:rows_per].reshape(chunk, width),
            w_all[span, rows_per : 2 * rows_per].reshape(chunk, width),
        )

    def feed(part, images, totals):
        span = slice(part * chunk_slots, (part + 1) * chunk_slots)
        tiles = b_all[span, 0, :].astype(BF16)
        bias_row = jnp.sum(
            jnp.where(owner_of, mm(tiles, unpack.astype(BF16)), 0.0), axis=0, keepdims=True
        )
        first, last = images

        def one(step, total):
            image = first + step if last > first else first - step
            up, down = feed_spans(part)
            before = mm_nt(n2[image], up) + bias_row
            hidden, slope = gelu_both(before)
            hidden_all[part, image] = hidden.astype(BF16)
            grad_before = (mm_nt(cot_all[image], down) * slope).astype(BF16)
            before_all[image] = grad_before
            if part == 0:
                grad_two[image] = mm(grad_before, up)
            else:
                grad_two[image] += mm(grad_before, up)
            return total + fold_rows(grad_before.astype(F32))

        return lax.fori_loop(0, abs(last - first) + 1, one, totals)

    def feed_result(part):
        @pl.loop(0, 4)
        def _(image):
            _, down = feed_spans(part)
            if part == 0:
                result[image] = mm(hidden_all[part, image], down)
            else:
                result[image] += mm(hidden_all[part, image], down)

    g_all, gb_all = s.g_all, s.gb_all

    def feed_weights(part, bias_total):
        first = part * chunk_slots
        span = slice(first, first + chunk_slots)

        for left, right, base in ((before_all, n2, 0), (hidden_all.at[part], cot_all, rows_per)):
            total = jnp.zeros((chunk, width), F32)
            for image in range(4):
                total += mm_tn(left[image], right[image])
            g_all[span, base : base + rows_per] = (
                total.astype(BF16).reshape(chunk_slots, rows_per, width)
            )
        bias_row = jnp.sum(bias_total, axis=0, keepdims=True)
        spread = jnp.where(owner_of, jnp.broadcast_to(bias_row, owner_of.shape), 0.0)
        high = spread.astype(BF16)
        low = (spread - high.astype(F32)).astype(BF16)
        packed = mm_nt(high, unpack.astype(BF16)) + mm_nt(low, unpack.astype(BF16))
        for slot in range(chunk_slots):
            gb_all[first + slot] = jnp.broadcast_to(packed[slot : slot + 1], (8, LANES))

    order = list(range(1, ring)) + [0]
    stores = []
    sum_y, sum_ring, sum_both, sum_last = {}, {}, {}, []
    first_rows, second_rows = pl.ds(0, rows_per), pl.ds(rows_per, rows_per)

    def sum_send_y(distance):
        slot = 2 * distance + 1
        sum_y[distance] = [
            links.send(g_all.at[slot, first_rows], s.ry.at[distance], ydev),
            links.send(gb_all.at[slot], s.ryb.at[distance], ydev),
        ]

    def sum_a_step(distance):
        for copy in sum_y[distance]:
            copy.wait_recv()
        mine = 2 * distance
        total = g_all[mine, 0:rows_per].astype(F32) + s.ry[distance].astype(F32)
        bias = gb_all[mine] + s.ryb[distance]
        if distance != 1:
            before = (distance + ring - 1) % ring
            for copy in sum_ring[before]:
                copy.wait_recv()
            total += s.rz_in[before].astype(F32)
            bias += s.rzb_in[before]
        if distance == 0:
            s.own_fc1[...] = total
            s.own_bias[...] = bias
            stores.append(loads.start(s.own_fc1, out_fc1))
            stores.append(loads.start(s.own_bias, out_bias))
        else:
            s.rz_out[distance] = total.astype(BF16)
            s.rzb_out[distance] = bias
            sum_ring[distance] = [
                links.send(s.rz_out.at[distance], s.rz_in.at[distance], ring_next),
                links.send(s.rzb_out.at[distance], s.rzb_in.at[distance], ring_next),
            ]

    def sum_b_step(distance):
        if distance == 1:
            source = g_all.at[pl.ds(2, 2), second_rows]
            sum_both[1] = links.send(source, s.rb_in.at[1], ring_next)
            return
        before = (distance + ring - 1) % ring
        sum_both[before].wait_recv()
        for line in range(2):
            total = g_all[2 * distance + line, rows_per:].astype(F32) + s.rb_in[before, line].astype(F32)
            if distance == 0 and line == 0:
                s.own_fc2[...] = total
            else:
                s.rb_out[distance, line] = total.astype(BF16)
        if distance == 0:
            sum_last.append(links.send(s.rb_out.at[0, 1], s.ry_last, ydev))
        else:
            sum_both[distance] = links.send(s.rb_out.at[distance], s.rb_in.at[distance], ring_next)

    def sum_b_end():
        sum_last[0].wait_recv()
        s.own_fc2[...] += s.ry_last[...].astype(F32)
        stores.append(loads.start(s.own_fc2, out_fc2))

    sums_done = [0, 1]

    def sum_a_until(steps):
        while sums_done[0] < min(steps, ring):
            sum_a_step(order[sums_done[0]])
            sums_done[0] += 1

    def sum_b_until(steps):
        while sums_done[1] < min(steps, ring):
            sum_b_step(order[sums_done[1]])
            sums_done[1] += 1

    def gather_wait(part):
        per = chunk_slots // 2
        gather_until((part + 1) * per - 1, 1)
        for distance in range(part * per, (part + 1) * per):
            for kind in range(2):
                for copy in gather_y[distance, kind]:
                    copy.wait_recv()

    part_out, part_in = s.part_out, s.part_in
    cross_out, cross_in = s.cross_out, s.cross_in
    part_sib, cross = {}, {}

    def hand_part(kind, place):
        total = (grad_two, result)[kind]
        part_out[kind, place] = total[(3, 1)[place]].astype(BF16)
        part_sib[kind, place] = links.send(part_out.at[kind, place], part_in.at[kind, place], sib)

    def hand_cross(kind):
        total = (grad_two, result)[kind]
        part_sib[kind, 0].wait_recv()
        cross_out[kind] = (total[2] + part_in[kind, 0].astype(F32)).astype(BF16)
        cross[kind] = links.send(cross_out.at[kind], cross_in.at[kind], xdev)

    gather_until(2, 1)
    gather_wait(0)
    n2_sib.wait_recv()
    cot_sib.wait_recv()
    no_bias = jnp.zeros((8, chunk), F32)
    bias_total = feed(0, (0, 0), no_bias)
    bias_total = feed(0, (1, 1), bias_total)
    gather_until(ring - 1, 0)
    n2_x.wait_recv()
    n2_far = links.send(n2.at[2], n2.at[3], sib)
    gather_until(ring - 1, 1)
    cot_far.wait_recv()
    bias_total = feed(0, (2, 2), bias_total)
    n2_far.wait_recv()
    bias_total = feed(0, (3, 3), bias_total)
    feed_weights(0, bias_total)
    sum_b_step(1)
    for distance in range(1, chunk_slots // 2):
        sum_send_y(distance)
    feed_result(0)
    if chunks == 2:
        gather_wait(1)
        bias_total = feed(1, (3, 3), no_bias)
        hand_part(0, 0)
        bias_total = feed(1, (2, 2), bias_total)
    else:
        hand_part(0, 0)
    hand_cross(0)
    if chunks == 2:
        bias_total = feed(1, (1, 0), bias_total)
    hand_part(0, 1)
    sum_a_until(1)
    if chunks == 2:
        feed_weights(1, bias_total)
    for distance in range(chunk_slots // 2, ring):
        sum_send_y(distance)
    sum_send_y(0)
    sum_b_until(2)
    if chunks == 2:
        feed_result(1)
    hand_part(1, 0)
    hand_part(1, 1)
    hand_cross(1)
    for image in range(2):
        s.n1_t[:, image * seq : (image + 1) * seq] = n1[image].T
    part_sib[0, 1].wait_recv()
    cross[0].wait_recv()
    grad_mid, grad_branch = stream, s.grad_branch

    def mid_back(step, totals):
        at = pl.ds(pl.multiple_of(step * block, block), block)
        grads = (
            grad_two[0, at, :] + part_in[0, 1, at, :].astype(F32) + cross_in[0, at, :].astype(F32)
        )
        unit_rows, scale = s.unit_two[at, :], s.scale_two[at, :]
        passed = cot_all[0, at, :].astype(F32)
        mid = passed + norm_back(grads, vecs[3:4, :], unit_rows, scale)
        grad_mid[at, :] = mid
        low = mid.astype(BF16)
        grad_branch[0, at, :] = low
        return (
            totals[0] + fold_rows(grads * unit_rows),
            totals[1] + fold_rows(grads),
            totals[2] + fold_rows(low.astype(F32)),
            totals[3] + fold_rows(passed),
        )

    empty = jnp.zeros((8, width), F32)
    gain_two_sum, shift_two_sum, out_bias_sum, fc2_bias_sum = lax.fori_loop(
        0, blocks, mid_back, (empty,) * 4
    )
    branch_back = links.send(grad_branch.at[0], grad_branch.at[1], sib)

    def mixed_back(image):
        grads = mm_nt(grad_branch[image], wout[...])
        for pair in range(pairs):
            s.grad_mixed[image, pair] = grads[:, pair * LANES : (pair + 1) * LANES].astype(BF16)

    grads_pair = s.grads_pair

    def attend_back(image, pair):
        queries, keys = s.q[image, pair], s.k[image, pair]
        values, grads = s.v[image, pair], s.grad_mixed[image, pair]
        keys_t = (keys * score_scale).T
        grad_values = jnp.zeros((seq, LANES), F32)
        grad_keys = jnp.zeros((seq, LANES), F32)
        grad_queries = []
        for half in range(2):
            probs = s.probs[image * 2 * pairs + pair * 2 + half]
            grads_half = grads * lane_half[half]
            grad_values += mm(probs.astype(BF16), grads_half)
            grad_probs = mm_nt(values, grads_half)
            inner = jnp.sum(grad_probs * probs, axis=0, keepdims=True)
            grad_scores = (probs * (grad_probs - inner)).astype(BF16)
            grad_keys += mm(grad_scores, queries * lane_scaled[half])
            grad_queries.append(
                mm(keys_t[half * HEAD_DIM : (half + 1) * HEAD_DIM], grad_scores)
            )
        grad_query = jnp.concatenate(grad_queries, axis=0).T
        for place, value in enumerate(
            (grad_query, grad_keys, grad_values)
        ):
            grads_pair[pair, image, :, place * LANES : (place + 1) * LANES] = value.astype(BF16)

    def rows_back(image):
        total = mm_nt(grads_pair[0, image], w_pair[0])
        for pair in range(1, pairs):
            total += mm_nt(grads_pair[pair, image], w_pair[pair])
        return total

    def weights_back(pair):
        both = grads_pair[pair].reshape(2 * seq, 3 * LANES)
        for base in range(0, width, 256):
            rows = slice(base, base + 256)
            ar[1 + pair, rows, :] = mm(s.n1_t[rows, :], both).astype(BF16)

    mixed_back(0)
    sum_a_until(2)
    sum_b_until(3)
    branch_back.wait_recv()
    mixed_back(1)

    ar = s.ar
    by_core = (one_dev, two_dev, p_one, p_two)
    flat = [
        (ar.at[item], s.ar_one.at[item], s.ar_two.at[item], s.ar_z.at[item],
         s.ar_rest.at[item], s.attn.at[item], width, by_core)
        for item in range(4)
    ]
    small_half = seq // 2
    small = (s.small, s.small_one, s.small_two, s.small_z, s.small_rest,
             s.small_all, small_half, by_core)
    items = flat + [small]
    stages = [dict() for _ in range(7)]

    def piece(item):
        total_rows = items[item][6]
        _, _, p_one, p_two = items[item][7]
        half, quarter, leaf = total_rows // 2, total_rows // 4, total_rows // 16
        at_one = pl.multiple_of(p_one * half, half)
        at_two = pl.multiple_of(at_one + p_two * quarter, quarter)
        return half, quarter, leaf, at_one, at_two

    def reduce_one(item):
        data, one = items[item][0], items[item][1]
        half, _, _, _, _ = piece(item)
        device, _, p_one, _ = items[item][7]
        other = pl.ds(pl.multiple_of((1 - p_one) * half, half), half)
        stages[0][item] = [links.send(data.at[other], one, device)]

    def reduce_two(item):
        data, one, two = items[item][:3]
        half, quarter, _, at_one, _ = piece(item)
        stages[0][item][0].wait_recv()
        mine = pl.ds(at_one, half)
        data[mine] = (data[mine].astype(F32) + one[...].astype(F32)).astype(data.dtype)
        _, device, _, p_two = items[item][7]
        other = pl.ds(pl.multiple_of(at_one + (1 - p_two) * quarter, quarter), quarter)
        stages[1][item] = [links.send(data.at[other], two, device)]

    def reduce_z(item):
        data, _, two, by_z = items[item][:4]
        _, quarter, leaf, _, at_two = piece(item)
        stages[1][item][0].wait_recv()
        mine = pl.ds(at_two, quarter)
        data[mine] = (data[mine].astype(F32) + two[...].astype(F32)).astype(data.dtype)
        stages[2][item] = [
            links.send(
                data.at[pl.ds(pl.multiple_of(at_two + ((zq + hop) % 4) * leaf, leaf), leaf)],
                by_z.at[hop - 1],
                zdev[hop],
            )
            for hop in range(1, 4)
        ]

    def spread_z(item):
        data, _, _, by_z, by_rest, done = items[item][:6]
        _, _, leaf, _, at_two = piece(item)
        for copy in stages[2][item]:
            copy.wait_recv()
        mine = pl.ds(pl.multiple_of(at_two + zq * leaf, leaf), leaf)
        total = data[mine].astype(F32)
        for hop in range(3):
            total += by_z[hop].astype(F32)
        if rest_count > 1:
            by_rest[0] = total.astype(data.dtype)
            copies = [
                links.send(by_rest.at[0], by_rest.at[hop], rdev[hop])
                for hop in range(1, rest_count)
            ]
            for copy in copies:
                copy.wait_recv()
            total = jnp.zeros(total.shape, F32)
            for owner in range(rest_count):
                total += by_rest[(rest - owner + rest_count) % rest_count].astype(F32)
        done[mine] = total.astype(done.dtype)
        stages[3][item] = [
            links.send(done.at[mine], done.at[mine], zdev[hop]) for hop in range(1, 4)
        ]

    def spread_two(item):
        done = items[item][5]
        _, quarter, _, _, at_two = piece(item)
        for copy in stages[3][item]:
            copy.wait_recv()
        mine = pl.ds(at_two, quarter)
        stages[4][item] = [links.send(done.at[mine], done.at[mine], items[item][7][1])]

    def spread_one(item):
        done = items[item][5]
        half, _, _, at_one, _ = piece(item)
        stages[4][item][0].wait_recv()
        mine = pl.ds(at_one, half)
        stages[5][item] = [links.send(done.at[mine], done.at[mine], items[item][7][0])]

    def finish(item):
        stages[5][item][0].wait_recv()
        if item < 4:
            stores.append(loads.start(s.attn.at[item], out_attn.at[item]))

    for half in range(2):
        at = slice(half * local, (half + 1) * local)
        total = mm(s.mixed_t[0], grad_branch[0, :, at]) + mm(
            s.mixed_t[1], grad_branch[1, :, at]
        )
        ar[0, at, :] = total.astype(BF16)
    reduce_one(0)
    for pair in range(pairs):
        attend_back(1, pair)
        attend_back(0, pair)
        weights_back(pair)
        reduce_one(1 + pair)
        if pair == 1:
            sum_a_until(3)
    s.rows_out[...] = rows_back(1).astype(BF16)
    rows_sib = links.send(s.rows_out, s.rows_in, sib)
    reduce_two(0)
    sum_b_until(ring)
    s.branch_own[...] = rows_back(0)
    reduce_two(1)
    reduce_z(0)
    rows_sib.wait_recv()

    def in_back(step, totals):
        at = pl.ds(pl.multiple_of(step * block, block), block)
        grads = (s.branch_own[at, :] + s.rows_in[at, :].astype(F32))
        unit_rows, scale = s.unit_one[at, :], s.scale_one[at, :]
        grad_mid[at, :] += norm_back(grads, vecs[0:1, :], unit_rows, scale)
        return (totals[0] + fold_rows(grads * unit_rows), totals[1] + fold_rows(grads))

    gain_one_sum, shift_one_sum = lax.fori_loop(0, blocks, in_back, (empty,) * 2)
    grad_in = grad_mid[...]
    high = grad_in.astype(BF16)
    low = (grad_in - high.astype(F32)).astype(BF16)
    placed = mm(pick[...], high) + mm(pick[...], low)
    s.own_tok[0] = placed[0:tok_rows]
    stores.append(loads.start(s.own_tok.at[0], out_tok.at[:, 0, :]))

    small_ref, small_own = s.small_full, s.small
    small_ref[...] = jnp.zeros(small_ref.shape, F32)
    part_width = small_ref.shape[1]
    parts = width // part_width
    for part in range(parts):
        small_ref[part * prompt_pad : part * prompt_pad + prompt_pad, :] = placed[
            tok_pad : tok_pad + prompt_pad, part * part_width : (part + 1) * part_width
        ]
    base = parts * prompt_pad
    sums = (gain_one_sum, shift_one_sum, out_bias_sum, gain_two_sum, shift_two_sum, fc2_bias_sum)
    for place, total in enumerate(sums):
        row = jnp.sum(total, axis=0, keepdims=True)
        for part in range(parts):
            at = base + place * parts + part
            small_ref[at : at + 1, :] = row[:, part * part_width : (part + 1) * part_width]
    base += len(sums) * parts
    for place in range(2):
        at = slice(2 * place * LANES, 2 * place * LANES + LANES)
        row = jnp.concatenate(
            [
                jnp.sum(
                    grads_pair[pair, 0, :, at].astype(F32) + grads_pair[pair, 1, :, at].astype(F32),
                    axis=0,
                    keepdims=True,
                )
                for pair in range(pairs)
            ],
            axis=1,
        )
        for head in range(2):
            chosen = row * (h if head == 1 else 1 - h).astype(F32)
            at = base + head * 4 + place * 2
            small_ref[at : at + 1, :] = chosen[:, 0:part_width]
            small_ref[at + 1 : at + 2, 0 : local - part_width] = chosen[:, part_width:local]
    theirs = pl.ds(pl.multiple_of((1 - h) * small_half, small_half), small_half)
    ours = pl.ds(pl.multiple_of(h * small_half, small_half), small_half)
    small_sib = links.send(small_ref.at[theirs], s.small_in.at[1], sib)
    small_sib.wait_recv()
    small_own[...] = small_ref[ours] + s.small_in[1]
    reduce_one(4)
    reduce_two(2)
    reduce_z(1)
    sum_a_until(ring)
    spread_z(0)
    reduce_two(3)
    reduce_z(2)
    sum_b_end()
    spread_z(1)
    spread_two(0)
    reduce_two(4)
    reduce_z(3)
    spread_z(2)
    spread_two(1)
    reduce_z(4)
    spread_one(0)
    spread_z(3)
    spread_z(4)
    spread_two(2)
    spread_one(1)
    part_sib[1, 1].wait_recv()
    cross[1].wait_recv()

    @pl.loop(0, blocks)
    def _(step):
        at = pl.ds(pl.multiple_of(step * block, block), block)
        row_ids = lax.broadcasted_iota(jnp.int32, (block, 1), 0) + step * block
        total = result[0, at, :] + part_in[1, 1, at, :].astype(F32) + cross_in[1, at, :].astype(F32)
        rows = middle[at, :] + (total + vecs[5:6, :])
        s.own_rows[0, at, :] = jnp.where(row_ids < limit, rows, 0.0).astype(BF16)

    stores.append(loads.start(s.own_rows, out_rows))
    spread_two(4)
    spread_two(3)
    spread_one(2)
    spread_one(4)
    spread_one(3)
    finish(0)
    finish(1)
    finish(4)
    final = s.small_out
    final[ours] = s.small_all[...]
    small_back = links.send(s.small_all, s.small_in.at[0], sib)
    finish(2)
    small_back.wait_recv()
    final[theirs] = s.small_in[0]
    final[base + 8 : base + 12, :] = jnp.where(h == 0, final[base : base + 4, :], final[base + 4 : base + 8, :])
    stores.append(loads.start(final, out_small))
    finish(3)
    links.drain()
    for copy in stores:
        copy.wait()


def finish_kernel(dims, *refs):
    it = iter(refs)
    rows_in, tok_in, attn_in, small_in, fc1_in, fc2_in, bias_in = (next(it) for _ in range(7))
    (
        layer_out, grad_tokens, grad_prompts, gain_one, shift_one, w_query, b_query, w_key,
        w_value, b_value, w_out, b_out, gain_two, shift_two, w_fc1, b_fc1, w_fc2, b_fc2,
    ) = (next(it) for _ in range(18))
    s = SimpleNamespace(**dict(zip(dims.finish, it)))
    width, local = dims.width, dims.local
    rows = w_fc1.shape[0]
    loads = Loads(s.load_sems)
    load_attn = [loads.start(attn_in.at[item], s.attn.at[item]) for item in range(4)]
    load_small = loads.start(small_in, s.small)
    load_bias = loads.start(bias_in, s.bias)
    passing = [(rows_in, s.rows, layer_out), (tok_in, s.tok, grad_tokens)]
    if rows == fc1_in.shape[0]:
        passing += [(fc1_in, s.fc1, w_fc1), (fc2_in, s.fc2, w_fc2)]
    passing = [(loads.start(source, held), held, target) for source, held, target in passing]
    stores = []
    if rows != fc1_in.shape[0]:
        for source, held, target in ((fc1_in, s.fc1, w_fc1), (fc2_in, s.fc2, w_fc2)):
            loads.start(source, held).wait()
            s.cut[...] = held[0:rows]
            loads.start(s.cut, target).wait()
    for item in range(4):
        load_attn[item].wait()
        if item == 0:
            s.wide[:, 0:local] = s.attn[0, 0:local].astype(F32)
            s.wide[:, local : 2 * local] = s.attn[0, local : 2 * local].astype(F32)
            stores.append(loads.start(s.wide, w_out))
            continue
        at = slice((item - 1) * LANES, item * LANES)
        for place in range(3):
            s.tall[place, :, at] = s.attn[item, :, place * LANES : (place + 1) * LANES].astype(F32)
    for place, target in enumerate((w_query, w_key, w_value)):
        stores.append(loads.start(s.tall.at[place], target))
    for load, held, target in passing:
        load.wait()
        stores.append(loads.start(held, target))
    load_small.wait()
    load_bias.wait()
    part_width = s.small.shape[1]
    parts = width // part_width
    for part in range(parts):
        at = slice(part * part_width, (part + 1) * part_width)
        s.prompts[:, at] = s.small[part * dims.prompt_pad : part * dims.prompt_pad + dims.prompt_rows]
    stores.append(loads.start(s.prompts, grad_prompts))
    base = parts * dims.prompt_pad
    for place, target in enumerate((gain_one, shift_one, b_out, gain_two, shift_two, b_fc2)):
        for part in range(parts):
            at = base + place * parts + part
            s.row[place : place + 1, part * part_width : (part + 1) * part_width] = s.small[at : at + 1]
        target[...] = s.row[place : place + 1, :].reshape(width)
    base += 6 * parts + 8
    for place, target in enumerate((b_query, b_value)):
        at = base + 2 * place
        s.row[6:7, 0:part_width] = s.small[at : at + 1]
        s.row[6:7, part_width : 2 * part_width] = s.small[at + 1 : at + 2]
        target[...] = s.row[6:7, 0:local].reshape(local)
    b_fc1[...] = s.bias[0:1, 0:rows].reshape(rows)
    for copy in stores:
        copy.wait()


def layer(dims, operands):
    seq, width, local = dims.seq, dims.width, dims.local
    n, ring, slots, rows_per = dims.n, dims.ring, dims.slots, dims.rows_per
    pairs = local // LANES
    chunk = dims.chunk_slots * rows_per
    rest_count = n // 16
    small_half = seq // 2
    part_width = 256
    copies = 6 * ring + 4 * ring + 40 + 5 * (10 + rest_count)
    vmem = pltpu.VMEM
    shared = 2 * rows_per
    scratch = dict(
        send_sems=pltpu.SemaphoreType.DMA((copies,)),
        recv_sems=pltpu.SemaphoreType.DMA((copies,)),
        w_all=vmem((slots, shared, width), BF16),
        b_all=vmem((slots, 8, LANES), F32),
        cot_all=vmem((4, seq, width), BF16),
        meta=vmem((2, 8, LANES), jnp.int32),
        load_sems=pltpu.SemaphoreType.DMA((36,)),
        kept=vmem((1, dims.patches), jnp.int32),
        tokens=vmem((1, dims.tok_rows, width), BF16),
        prompts=vmem((dims.prompt_rows, width), BF16),
        gain_one=vmem((width,), BF16),
        shift_one=vmem((width,), BF16),
        b_query=vmem((local,), BF16),
        b_value=vmem((local,), BF16),
        b_out=vmem((width,), BF16),
        gain_two=vmem((width,), BF16),
        shift_two=vmem((width,), BF16),
        b_fc1=vmem((dims.rows,), BF16),
        b_fc2=vmem((width,), BF16),
        vecs=vmem((8, width), F32),
        w_pair=vmem((pairs, width, 3 * LANES), BF16),
        wout=vmem((local, width), BF16),
        unit_one=vmem((seq, width), F32),
        unit_two=vmem((seq, width), F32),
        scale_one=vmem((seq, 1), F32),
        scale_two=vmem((seq, 1), F32),
        own_rows=vmem((1, seq, width), BF16),
        own_tok=vmem((1, dims.tok_rows, width), F32),
        own_fc1=vmem((rows_per, width), F32),
        own_fc2=vmem((rows_per, width), F32),
        own_bias=vmem((8, LANES), F32),
        attn=vmem((4, width, local), BF16),
        src=vmem((dims.tok_pad + dims.prompt_pad, width), BF16),
        pick=vmem((dims.tok_pad + dims.prompt_pad, seq), BF16),
        idx=vmem((8, seq), jnp.int32),
        stream=vmem((seq, width), F32),
        middle=vmem((seq, width), F32),
        n1=vmem((2, seq, width), BF16),
        n2=vmem((4, seq, width), BF16),
        q=vmem((2, pairs, seq, LANES), BF16),
        k=vmem((2, pairs, seq, LANES), BF16),
        v=vmem((2, pairs, seq, LANES), BF16),
        probs=vmem((4 * pairs, seq, seq), F32),
        mixed_t=vmem((2, local, seq), BF16),
        branch_out=vmem((seq, width), F32),
        branch_in=vmem((seq, width), F32),
        branch_own=vmem((seq, width), F32),
        hidden=vmem((slots // dims.chunk_slots, 4, seq, chunk), BF16),
        grad_before=vmem((4, seq, chunk), BF16),
        result=vmem((4, seq, width), F32),
        grad_two=vmem((4, seq, width), F32),
        part_out=vmem((2, 2, seq, width), BF16),
        part_in=vmem((2, 2, seq, width), BF16),
        cross_out=vmem((2, seq, width), BF16),
        cross_in=vmem((2, seq, width), BF16),
        g_all=vmem((slots, shared, width), BF16),
        gb_all=vmem((slots, 8, LANES), F32),
        ry=vmem((ring, rows_per, width), BF16),
        ry_last=vmem((rows_per, width), BF16),
        rb_out=vmem((ring, 2, rows_per, width), BF16),
        rb_in=vmem((ring, 2, rows_per, width), BF16),
        n1_t=vmem((width, 2 * seq), BF16),
        ryb=vmem((ring, 8, LANES), F32),
        rz_out=vmem((ring, rows_per, width), BF16),
        rzb_out=vmem((ring, 8, LANES), F32),
        rz_in=vmem((ring, rows_per, width), BF16),
        rzb_in=vmem((ring, 8, LANES), F32),
        grad_branch=vmem((2, seq, width), BF16),
        grad_mixed=vmem((2, pairs, seq, LANES), BF16),
        grads_pair=vmem((pairs, 2, seq, 3 * LANES), BF16),
        rows_out=vmem((seq, width), BF16),
        rows_in=vmem((seq, width), BF16),
        ar=vmem((4, width, local), BF16),
        ar_one=vmem((4, width // 2, local), BF16),
        ar_two=vmem((4, width // 4, local), BF16),
        ar_z=vmem((4, 3, width // 16, local), BF16),
        ar_rest=vmem((4, rest_count, width // 16, local), BF16),
        small_full=vmem((seq, part_width), F32),
        small_out=vmem((seq, part_width), F32),
        small_in=vmem((2, small_half, part_width), F32),
        small=vmem((small_half, part_width), F32),
        small_one=vmem((small_half // 2, part_width), F32),
        small_two=vmem((small_half // 4, part_width), F32),
        small_z=vmem((3, small_half // 16, part_width), F32),
        small_rest=vmem((rest_count, small_half // 16, part_width), F32),
        small_all=vmem((small_half, part_width), F32),
    )
    dims = SimpleNamespace(**vars(dims), scratch=tuple(scratch))
    anywhere = pl.BlockSpec(memory_space=pl.ANY)
    shape = jax.ShapeDtypeStruct
    return pl.pallas_call(
        functools.partial(layer_kernel, dims),
        out_shape=(
            shape((1, seq, width), BF16),
            shape((dims.tok_rows, 1, width), F32),
            shape((4, width, local), BF16),
            shape((seq, part_width), F32),
            shape((rows_per, width), F32),
            shape((rows_per, width), F32),
            shape((8, LANES), F32),
        ),
        in_specs=[pl.BlockSpec(memory_space=pltpu.SMEM)] + [anywhere] * (len(operands) - 1),
        out_specs=[anywhere] * 7,
        scratch_shapes=list(scratch.values()),
        compiler_params=pltpu.CompilerParams(
            collective_id=0, has_side_effects=True, vmem_limit_bytes=63 * 2**20
        ),
    )(*operands)


def finish(dims, results):
    seq, width, local, rows = dims.seq, dims.width, dims.local, dims.rows
    vmem = pltpu.VMEM
    scratch = dict(
        load_sems=pltpu.SemaphoreType.DMA((28,)),
        attn=vmem((4, width, local), BF16),
        wide=vmem((local, width), F32),
        tall=vmem((3, width, local), F32),
        small=vmem(results[3].shape, F32),
        bias=vmem((8, LANES), F32),
        prompts=vmem((dims.prompt_rows, width), F32),
        row=vmem((8, width), F32),
        rows=vmem((1, seq, width), BF16),
        tok=vmem((dims.tok_rows, 1, width), F32),
        fc1=vmem((dims.rows_per, width), F32),
        fc2=vmem((dims.rows_per, width), F32),
        cut=vmem((rows, width), F32),
    )
    dims = SimpleNamespace(**vars(dims), finish=tuple(scratch))
    anywhere = pl.BlockSpec(memory_space=pl.ANY)
    whole = pl.BlockSpec(memory_space=pltpu.VMEM)

    def out(*sizes, dtype=F32):
        return jax.ShapeDtypeStruct(sizes, dtype)

    shapes = (
        out(1, seq, width, dtype=BF16), out(dims.tok_rows, 1, width), out(dims.prompt_rows, width),
        out(width), out(width), out(width, local), out(local), out(width, local),
        out(width, local), out(local), out(local, width), out(width), out(width), out(width),
        out(rows, width), out(rows), out(rows, width), out(width),
    )
    return pl.pallas_call(
        functools.partial(finish_kernel, dims),
        out_shape=shapes,
        in_specs=[anywhere] * 7,
        out_specs=[whole if len(shape.shape) == 1 else anywhere for shape in shapes],
        scratch_shapes=list(scratch.values()),
        compiler_params=pltpu.CompilerParams(vmem_limit_bytes=60 * 2**20),
    )(*results)


def body(n, *arguments):
    (
        tokens, kept_index, kept_count, prompts, gain_one, shift_one, w_query, b_query, w_key,
        w_value, b_value, w_out, b_out, gain_two, shift_two, w_fc1, b_fc1, w_fc2, b_fc2, cotangent,
    ) = arguments
    seq, width = cotangent.shape[1:]
    local = w_query.shape[1]
    rows = w_fc1.shape[0]
    rows_per = round_up(rows, 16)
    ring = n // 4
    slots = 2 * ring
    halves = slots // 2
    chunk_slots = halves if (halves % 2 == 0 and halves * rows_per % LANES == 0) else slots
    tok_rows, prompt_rows = tokens.shape[1], prompts.shape[0]
    dims = SimpleNamespace(
        n=n, ring=ring, slots=slots, chunk_slots=chunk_slots, rows_per=rows_per, rows=rows, seq=seq,
        width=width, local=local, tok_rows=tok_rows, tok_pad=round_up(tok_rows, 16),
        prompt_rows=prompt_rows, prompt_pad=round_up(prompt_rows, 16),
        patches=kept_index.shape[1],
    )
    if rows_per != rows:
        spare = ((0, rows_per - rows), (0, 0))
        w_fc1, w_fc2 = jnp.pad(w_fc1, spare), jnp.pad(w_fc2, spare)
    operands = (
        kept_count, tokens, kept_index, prompts, w_fc1, w_fc2, cotangent, w_query, w_key, w_value,
        w_out, gain_one, shift_one, b_query, b_value, b_out, gain_two, shift_two, b_fc1, b_fc2,
    )
    outs = list(finish(dims, layer(dims, operands)))
    outs[1] = outs[1].transpose(1, 0, 2)
    return tuple(outs)


def solution(mesh):
    batch, head = mesh.axis_names
    both = (batch, head)
    placed = (
        P(both, None, None), P(both, None), P(both), P(), P(), P(), P(None, head), P(head),
        P(None, head), P(None, head), P(head), P(head, None), P(), P(), P(),
        P(both, None), P(both), P(both, None), P(), P(both, None, None),
    )
    return jax.shard_map(
        functools.partial(body, mesh.shape[batch]),
        mesh=mesh,
        in_specs=placed,
        out_specs=(
            P(both, None, None), P(both, None, None), P(), P(), P(), P(None, head), P(head),
            P(None, head), P(None, head), P(head), P(head, None), P(), P(), P(),
            P(both, None), P(both), P(both, None), P(),
        ),
        check_vma=False,
    )
```

time: 160 us -> 119 us (0.74)
  Pallas kernels: 136 us -> 117 us
  local copies, waits for them, and re-layouts: 17 us -> 0 us
  other arithmetic: 5.06 us -> 0 us
    pallas_call x1 -> x2, Pallas kernels: 136 us -> 117 us  [the longest x1 112 us: layer(): pl.pallas_call(functools.partial(layer_kernel, dims), out_shape=(shape((1...]
    squeeze x9 -> x0, local copies, waits for them, and re-layouts: 6.73 us -> none  [the longest x1 1.87 us: body(): grads[3]]
    unnamed x12 -> x0, local copies, waits for them, and re-layouts: 4.75 us -> none
    another operation x9 -> x0, local copies, waits for them, and re-layouts: 4.17 us -> none  [body(): jnp.stack([gain_one, shift_one, b_out, gain_two, shift_two, b_fc2, jnp.co...]
    convert_element_type x2 -> x0, other arithmetic: 2.58 us -> none  [the longest x1 1.97 us: body(): grads = out_attn.astype(F32)]
    concatenate x3 -> x0, other arithmetic: 2.48 us -> none  [the longest x1 1.1 us: body(): grad_out = jnp.concatenate([grads[0, :local], grads[0, local:]], axis=1)]
where the time goes in v2:
time: 119 us; the launch traced here: 118 us
  Pallas kernels  117 us (98%)
  between operations  1.48 us (1%)
    pallas_call x1, Pallas kernels, layer(): pl.pallas_call(functools.partial(layer_kernel, dims), out_shape=(shape((1...  112 us
    pallas_call x1, Pallas kernels, finish(): pl.pallas_call(functools.partial(finish_kernel, dims), out_shape=shapes,...  4.86 us

profile of v2, /device:TPU:0, one launch (start us, length us, event | category | flops | bytes accessed | tf_op | source)
XLA Modules:
  0.0 118.4 jit_solution(7603464259901311733)
XLA Ops:
  1.3 112.0 %shard_map.331 = (bf16[1,256,768]{2,1,0:T(8,128)(2,1)}, f32[197,1,768]{2,1,0:T(1,128)}, bf16[4,768,384]{2,1,0:T(8,128)(2,1)}, f32[256,256]{1,0:T(8,128)}, f32[96...) custom-call(s32[1]{0:T(128)S(6)} %copy.38.refs_0_, bf16[1,197,768]{2,1,0:T(8,128)(2,1)} %refs_1_.1, ...), custom_call_target="tpu_custom_call" | custom-call | tf_op jit(solution)/shard_map/pallas_call | solution.py:1035
  113.4 4.9 %shard_map.332 = (bf16[1,256,768]{2,1,0:T(8,128)(2,1)}, f32[197,1,768]{2,1,0:T(1,128)}, f32[50,768]{1,0:T(8,128)}, f32[768]{0:T(1024)}, f32[768]{0:T(1024)}, /*i...) custom-call(bf16[1,256,768]{2,1,0:T(8,128)(2,1)} %get-tuple-element., ...), custom_call_target="tpu_custom_call" | custom-call | tf_op jit(solution)/shard_map/pallas_call | solution.py:1086

commit v3 on v2

--- a/solution.py
+++ b/solution.py
@@ -70,6 +70,18 @@
 
 VECTORS = (
     "gain_one", "shift_one", "b_query", "b_value", "b_out", "gain_two", "shift_two", "b_fc1", "b_fc2",
+)
+
+
+LATE_SUM = (8, 1)
+REDUCE_ORDER = (
+    (0, 0), (-1, 0), (3, 0), (-2, 0), (5, 0), (1, 0), (-3, 0), (4, 0), (7, 0), (3, 1), (0, 1),
+    (5, 1), (2, 0), (1, 1), (3, 2), (0, 2), (4, 1), (5, 2), (1, 2), (3, 3), (-4, 0), (7, 1),
+    (6, 0), (0, 3), (1, 3), (7, 2), (4, 2), (2, 1), (3, 4), (-5, 0), (1, 4), (5, 3), (0, 4),
+    (6, 1), (-6, 0), (7, 3), (2, 2), (-7, 0), (4, 3), (8, 0), (3, 5), (1, 5), (5, 4), (7, 4),
+    (6, 2), (-8, 0), (8, 1), (2, 3), (0, 5), (6, 3), (5, 5), (4, 4), (8, 2), (2, 4), (7, 5),
+    (6, 4), (3, 6), (4, 5), (8, 3), (2, 5), (7, 6), (8, 4), (5, 6), (6, 5), (0, 6), (4, 6), (8, 5),
+    (6, 6), (1, 6), (2, 6), (8, 6),
 )
 
 
@@ -215,7 +227,7 @@
     b_all[0] = jnp.broadcast_to(vecs[7:8, 0:LANES], (8, LANES))
     load_cot.wait()
 
-    @pl.loop(0, blocks)
+    @pl.loop(0, blocks, unroll=4)
     def _(step):
         at = pl.ds(pl.multiple_of(step * block, block), block)
         row_ids = lax.broadcasted_iota(jnp.int32, (block, 1), 0) + step * block
@@ -231,7 +243,7 @@
 
     n1 = s.n1
 
-    @pl.loop(0, blocks)
+    @pl.loop(0, blocks, unroll=4)
     def _(step):
         at = pl.ds(pl.multiple_of(step * block, block), block)
         unit_rows, s.scale_one[at, :] = normalise(stream[at, :])
@@ -300,8 +312,7 @@
     def attend(image, first, last):
         key_bias = jnp.where(key_ids < s.meta[image, 0:1, 0:1], 0.0, -1e30).astype(BF16)
 
-        @pl.loop(first, last)
-        def _(pair):
+        for pair in range(first, last):
             queries, keys = s.q[image, pair], s.k[image, pair]
             values_t = s.v[image, pair].T
             for half in range(2):
@@ -313,7 +324,7 @@
                 probs = weights * (1.0 / jnp.sum(weights, axis=0, keepdims=True))
                 s.probs[image * 2 * pairs + pair * 2 + half] = probs
                 mixed_t = mm(values_t[half * HEAD_DIM : (half + 1) * HEAD_DIM], probs.astype(BF16))
-                at = pl.ds(pl.multiple_of(pair * LANES + half * HEAD_DIM, HEAD_DIM), HEAD_DIM)
+                at = pl.ds(pair * LANES + half * HEAD_DIM, HEAD_DIM)
                 s.mixed_t[image, at, :] = mixed_t.astype(BF16)
 
     for copy in load_weights:
@@ -332,7 +343,7 @@
     branch_sib.wait_recv()
     middle, n2 = s.middle, s.n2
 
-    @pl.loop(0, blocks)
+    @pl.loop(0, blocks, unroll=4)
     def _(step):
         at = pl.ds(pl.multiple_of(step * block, block), block)
         rows = stream[at, :] + (s.branch_own[at, :] + s.branch_in[at, :] + vecs[2:3, :])
@@ -372,11 +383,8 @@
         bias_row = jnp.sum(
             jnp.where(owner_of, mm(tiles, unpack.astype(BF16)), 0.0), axis=0, keepdims=True
         )
-        first, last = images
-
-        def one(step, total):
-            image = first + step if last > first else first - step
-            up, down = feed_spans(part)
+        up, down = feed_spans(part)
+        for image in images:
             before = mm_nt(n2[image], up) + bias_row
             hidden, slope = gelu_both(before)
             hidden_all[part, image] = hidden.astype(BF16)
@@ -386,9 +394,8 @@
                 grad_two[image] = mm(grad_before, up)
             else:
                 grad_two[image] += mm(grad_before, up)
-            return total + fold_rows(grad_before.astype(F32))
-
-        return lax.fori_loop(0, abs(last - first) + 1, one, totals)
+            totals += fold_rows(grad_before.astype(F32))
+        return totals
 
     def feed_result(part):
         @pl.loop(0, 4)
@@ -520,16 +527,15 @@
     n2_sib.wait_recv()
     cot_sib.wait_recv()
     no_bias = jnp.zeros((8, chunk), F32)
-    bias_total = feed(0, (0, 0), no_bias)
-    bias_total = feed(0, (1, 1), bias_total)
+    bias_total = feed(0, (0, 1), no_bias)
     gather_until(ring - 1, 0)
     n2_x.wait_recv()
     n2_far = links.send(n2.at[2], n2.at[3], sib)
     gather_until(ring - 1, 1)
     cot_far.wait_recv()
-    bias_total = feed(0, (2, 2), bias_total)
+    bias_total = feed(0, (2,), bias_total)
     n2_far.wait_recv()
-    bias_total = feed(0, (3, 3), bias_total)
+    bias_total = feed(0, (3,), bias_total)
     feed_weights(0, bias_total)
     sum_b_step(1)
     for distance in range(1, chunk_slots // 2):
@@ -537,14 +543,14 @@
     feed_result(0)
     if chunks == 2:
         gather_wait(1)
-        bias_total = feed(1, (3, 3), no_bias)
+        bias_total = feed(1, (3,), no_bias)
         hand_part(0, 0)
-        bias_total = feed(1, (2, 2), bias_total)
+        bias_total = feed(1, (2,), bias_total)
     else:
         hand_part(0, 0)
     hand_cross(0)
     if chunks == 2:
-        bias_total = feed(1, (1, 0), bias_total)
+        bias_total = feed(1, (0, 1), bias_total)
     hand_part(0, 1)
     sum_a_until(1)
     if chunks == 2:
@@ -560,6 +566,7 @@
     hand_cross(1)
     for image in range(2):
         s.n1_t[:, image * seq : (image + 1) * seq] = n1[image].T
+    sum_a_until(2)
     part_sib[0, 1].wait_recv()
     cross[0].wait_recv()
     grad_mid, grad_branch = stream, s.grad_branch
@@ -584,7 +591,7 @@
 
     empty = jnp.zeros((8, width), F32)
     gain_two_sum, shift_two_sum, out_bias_sum, fc2_bias_sum = lax.fori_loop(
-        0, blocks, mid_back, (empty,) * 4
+        0, blocks, mid_back, (empty,) * 4, unroll=4
     )
     branch_back = links.send(grad_branch.at[0], grad_branch.at[1], sib)
 
@@ -632,17 +639,18 @@
             ar[1 + pair, rows, :] = mm(s.n1_t[rows, :], both).astype(BF16)
 
     mixed_back(0)
-    sum_a_until(2)
-    sum_b_until(3)
+    attend_back(0, 0)
     branch_back.wait_recv()
     mixed_back(1)
 
     ar = s.ar
     by_core = (one_dev, two_dev, p_one, p_two)
+    cuts = [(array, lanes) for array in range(4) for lanes in (pl.ds(0, 256), pl.ds(256, local - 256))]
     flat = [
-        (ar.at[item], s.ar_one.at[item], s.ar_two.at[item], s.ar_z.at[item],
-         s.ar_rest.at[item], s.attn.at[item], width, by_core)
-        for item in range(4)
+        (ar.at[array, :, lanes], s.ar_one.at[array, :, lanes], s.ar_two.at[array, :, lanes],
+         s.ar_z.at[array, :, :, lanes], s.ar_rest.at[array, :, :, lanes], s.attn.at[array, :, lanes],
+         width, by_core)
+        for array, lanes in cuts
     ]
     small_half = seq // 2
     small = (s.small, s.small_one, s.small_two, s.small_z, s.small_rest,
@@ -732,8 +740,9 @@
 
     def finish(item):
         stages[5][item][0].wait_recv()
-        if item < 4:
-            stores.append(loads.start(s.attn.at[item], out_attn.at[item]))
+        if item < len(cuts):
+            array, lanes = cuts[item]
+            stores.append(loads.start(s.attn.at[array, :, lanes], out_attn.at[array, :, lanes]))
 
     for half in range(2):
         at = slice(half * local, (half + 1) * local)
@@ -741,126 +750,129 @@
             s.mixed_t[1], grad_branch[1, :, at]
         )
         ar[0, at, :] = total.astype(BF16)
-    reduce_one(0)
-    for pair in range(pairs):
+    def out_back():
+        part_sib[1, 1].wait_recv()
+        cross[1].wait_recv()
+
+        @pl.loop(0, blocks, unroll=4)
+        def _(step):
+            at = pl.ds(pl.multiple_of(step * block, block), block)
+            row_ids = lax.broadcasted_iota(jnp.int32, (block, 1), 0) + step * block
+            total = result[0, at, :] + part_in[1, 1, at, :].astype(F32) + cross_in[1, at, :].astype(F32)
+            rows = middle[at, :] + (total + vecs[5:6, :])
+            s.own_rows[0, at, :] = jnp.where(row_ids < limit, rows, 0.0).astype(BF16)
+
+        stores.append(loads.start(s.own_rows, out_rows))
+
+    def pair_back(pair):
+        if pair == 0:
+            sum_b_until(3)
         attend_back(1, pair)
-        attend_back(0, pair)
+        if pair > 0:
+            attend_back(0, pair)
         weights_back(pair)
-        reduce_one(1 + pair)
         if pair == 1:
             sum_a_until(3)
-    s.rows_out[...] = rows_back(1).astype(BF16)
-    rows_sib = links.send(s.rows_out, s.rows_in, sib)
-    reduce_two(0)
-    sum_b_until(ring)
-    s.branch_own[...] = rows_back(0)
-    reduce_two(1)
-    reduce_z(0)
-    rows_sib.wait_recv()
-
-    def in_back(step, totals):
-        at = pl.ds(pl.multiple_of(step * block, block), block)
-        grads = (s.branch_own[at, :] + s.rows_in[at, :].astype(F32))
-        unit_rows, scale = s.unit_one[at, :], s.scale_one[at, :]
-        grad_mid[at, :] += norm_back(grads, vecs[0:1, :], unit_rows, scale)
-        return (totals[0] + fold_rows(grads * unit_rows), totals[1] + fold_rows(grads))
-
-    gain_one_sum, shift_one_sum = lax.fori_loop(0, blocks, in_back, (empty,) * 2)
-    grad_in = grad_mid[...]
-    high = grad_in.astype(BF16)
-    low = (grad_in - high.astype(F32)).astype(BF16)
-    placed = mm(pick[...], high) + mm(pick[...], low)
-    s.own_tok[0] = placed[0:tok_rows]
-    stores.append(loads.start(s.own_tok.at[0], out_tok.at[:, 0, :]))
-
-    small_ref, small_own = s.small_full, s.small
-    small_ref[...] = jnp.zeros(small_ref.shape, F32)
-    part_width = small_ref.shape[1]
-    parts = width // part_width
-    for part in range(parts):
-        small_ref[part * prompt_pad : part * prompt_pad + prompt_pad, :] = placed[
-            tok_pad : tok_pad + prompt_pad, part * part_width : (part + 1) * part_width
-        ]
-    base = parts * prompt_pad
-    sums = (gain_one_sum, shift_one_sum, out_bias_sum, gain_two_sum, shift_two_sum, fc2_bias_sum)
-    for place, total in enumerate(sums):
-        row = jnp.sum(total, axis=0, keepdims=True)
-        for part in range(parts):
-            at = base + place * parts + part
-            small_ref[at : at + 1, :] = row[:, part * part_width : (part + 1) * part_width]
-    base += len(sums) * parts
-    for place in range(2):
-        at = slice(2 * place * LANES, 2 * place * LANES + LANES)
-        row = jnp.concatenate(
-            [
-                jnp.sum(
-                    grads_pair[pair, 0, :, at].astype(F32) + grads_pair[pair, 1, :, at].astype(F32),
-                    axis=0,
-                    keepdims=True,
-                )
-                for pair in range(pairs)
-            ],
-            axis=1,
-        )
-        for head in range(2):
-            chosen = row * (h if head == 1 else 1 - h).astype(F32)
-            at = base + head * 4 + place * 2
-            small_ref[at : at + 1, :] = chosen[:, 0:part_width]
-            small_ref[at + 1 : at + 2, 0 : local - part_width] = chosen[:, part_width:local]
+
+    held = SimpleNamespace()
+
+    def rows_hand():
+        s.rows_out[...] = rows_back(1).astype(BF16)
+        held.rows_sib = links.send(s.rows_out, s.rows_in, sib)
+
+    def rows_keep():
+        s.branch_own[...] = rows_back(0)
+
+    def norm_one_back():
+        held.rows_sib.wait_recv()
+
+        def in_back(step, totals):
+            at = pl.ds(pl.multiple_of(step * block, block), block)
+            grads = (s.branch_own[at, :] + s.rows_in[at, :].astype(F32))
+            unit_rows, scale = s.unit_one[at, :], s.scale_one[at, :]
+            grad_mid[at, :] += norm_back(grads, vecs[0:1, :], unit_rows, scale)
+            return (totals[0] + fold_rows(grads * unit_rows), totals[1] + fold_rows(grads))
+
+        held.sums = lax.fori_loop(0, blocks, in_back, (empty,) * 2, unroll=4)
+        sum_a_until(ring)
+
     theirs = pl.ds(pl.multiple_of((1 - h) * small_half, small_half), small_half)
     ours = pl.ds(pl.multiple_of(h * small_half, small_half), small_half)
-    small_sib = links.send(small_ref.at[theirs], s.small_in.at[1], sib)
-    small_sib.wait_recv()
-    small_own[...] = small_ref[ours] + s.small_in[1]
-    reduce_one(4)
-    reduce_two(2)
-    reduce_z(1)
-    sum_a_until(ring)
-    spread_z(0)
-    reduce_two(3)
-    reduce_z(2)
-    sum_b_end()
-    spread_z(1)
-    spread_two(0)
-    reduce_two(4)
-    reduce_z(3)
-    spread_z(2)
-    spread_two(1)
-    reduce_z(4)
-    spread_one(0)
-    spread_z(3)
-    spread_z(4)
-    spread_two(2)
-    spread_one(1)
-    part_sib[1, 1].wait_recv()
-    cross[1].wait_recv()
-
-    @pl.loop(0, blocks)
-    def _(step):
-        at = pl.ds(pl.multiple_of(step * block, block), block)
-        row_ids = lax.broadcasted_iota(jnp.int32, (block, 1), 0) + step * block
-        total = result[0, at, :] + part_in[1, 1, at, :].astype(F32) + cross_in[1, at, :].astype(F32)
-        rows = middle[at, :] + (total + vecs[5:6, :])
-        s.own_rows[0, at, :] = jnp.where(row_ids < limit, rows, 0.0).astype(BF16)
-
-    stores.append(loads.start(s.own_rows, out_rows))
-    spread_two(4)
-    spread_two(3)
-    spread_one(2)
-    spread_one(4)
-    spread_one(3)
-    finish(0)
-    finish(1)
-    finish(4)
+    small_ref, small_own = s.small_full, s.small
+    small_base = (width // small_ref.shape[1]) * prompt_pad + 6 * (width // small_ref.shape[1])
+
+    def place_small():
+        gain_one_sum, shift_one_sum = held.sums
+        grad_in = grad_mid[...]
+        high = grad_in.astype(BF16)
+        low = (grad_in - high.astype(F32)).astype(BF16)
+        placed = mm(pick[...], high) + mm(pick[...], low)
+        s.own_tok[0] = placed[0:tok_rows]
+        stores.append(loads.start(s.own_tok.at[0], out_tok.at[:, 0, :]))
+
+        small_ref[...] = jnp.zeros(small_ref.shape, F32)
+        part_width = small_ref.shape[1]
+        parts = width // part_width
+        for part in range(parts):
+            small_ref[part * prompt_pad : part * prompt_pad + prompt_pad, :] = placed[
+                tok_pad : tok_pad + prompt_pad, part * part_width : (part + 1) * part_width
+            ]
+        base = parts * prompt_pad
+        sums = (gain_one_sum, shift_one_sum, out_bias_sum, gain_two_sum, shift_two_sum, fc2_bias_sum)
+        for place, total in enumerate(sums):
+            row = jnp.sum(total, axis=0, keepdims=True)
+            for part in range(parts):
+                at = base + place * parts + part
+                small_ref[at : at + 1, :] = row[:, part * part_width : (part + 1) * part_width]
+        base += len(sums) * parts
+        for place in range(2):
+            at = slice(2 * place * LANES, 2 * place * LANES + LANES)
+            row = jnp.concatenate(
+                [
+                    jnp.sum(
+                        grads_pair[pair, 0, :, at].astype(F32) + grads_pair[pair, 1, :, at].astype(F32),
+                        axis=0,
+                        keepdims=True,
+                    )
+                    for pair in range(pairs)
+                ],
+                axis=1,
+            )
+            for head in range(2):
+                chosen = row * (h if head == 1 else 1 - h).astype(F32)
+                at = base + head * 4 + place * 2
+                small_ref[at : at + 1, :] = chosen[:, 0:part_width]
+                small_ref[at + 1 : at + 2, 0 : local - part_width] = chosen[:, part_width:local]
+        held.small_sib = links.send(small_ref.at[theirs], s.small_in.at[1], sib)
+        sum_b_until(ring)
+
+    def reduce_small():
+        held.small_sib.wait_recv()
+        small_own[...] = small_ref[ours] + s.small_in[1]
+
+    blocks_beside = [
+        functools.partial(pair_back, 0), functools.partial(pair_back, 1), functools.partial(pair_back, 2),
+        rows_hand, rows_keep, norm_one_back, place_small, out_back,
+    ]
+    steps = [reduce_one, reduce_two, reduce_z, spread_z, spread_two, spread_one, finish]
+    for item, stage in REDUCE_ORDER:
+        if item < 0:
+            blocks_beside[-1 - item]()
+        else:
+            if stage == 0 and item == len(cuts):
+                reduce_small()
+            steps[stage](item)
+            if (item, stage) == LATE_SUM:
+                sum_b_end()
     final = s.small_out
     final[ours] = s.small_all[...]
     small_back = links.send(s.small_all, s.small_in.at[0], sib)
-    finish(2)
     small_back.wait_recv()
     final[theirs] = s.small_in[0]
-    final[base + 8 : base + 12, :] = jnp.where(h == 0, final[base : base + 4, :], final[base + 4 : base + 8, :])
+    final[small_base + 8 : small_base + 12, :] = jnp.where(
+        h == 0, final[small_base : small_base + 4, :], final[small_base + 4 : small_base + 8, :]
+    )
     stores.append(loads.start(final, out_small))
-    finish(3)
     links.drain()
     for copy in stores:
         copy.wait()
@@ -877,34 +889,15 @@
     width, local = dims.width, dims.local
     rows = w_fc1.shape[0]
     loads = Loads(s.load_sems)
-    load_attn = [loads.start(attn_in.at[item], s.attn.at[item]) for item in range(4)]
     load_small = loads.start(small_in, s.small)
     load_bias = loads.start(bias_in, s.bias)
+    load_attn = [loads.start(attn_in.at[array], s.attn.at[array]) for array in (1, 2, 3, 0)]
     passing = [(rows_in, s.rows, layer_out), (tok_in, s.tok, grad_tokens)]
-    if rows == fc1_in.shape[0]:
+    whole_shards = rows == fc1_in.shape[0]
+    if whole_shards:
         passing += [(fc1_in, s.fc1, w_fc1), (fc2_in, s.fc2, w_fc2)]
     passing = [(loads.start(source, held), held, target) for source, held, target in passing]
     stores = []
-    if rows != fc1_in.shape[0]:
-        for source, held, target in ((fc1_in, s.fc1, w_fc1), (fc2_in, s.fc2, w_fc2)):
-            loads.start(source, held).wait()
-            s.cut[...] = held[0:rows]
-            loads.start(s.cut, target).wait()
-    for item in range(4):
-        load_attn[item].wait()
-        if item == 0:
-            s.wide[:, 0:local] = s.attn[0, 0:local].astype(F32)
-            s.wide[:, local : 2 * local] = s.attn[0, local : 2 * local].astype(F32)
-            stores.append(loads.start(s.wide, w_out))
-            continue
-        at = slice((item - 1) * LANES, item * LANES)
-        for place in range(3):
-            s.tall[place, :, at] = s.attn[item, :, place * LANES : (place + 1) * LANES].astype(F32)
-    for place, target in enumerate((w_query, w_key, w_value)):
-        stores.append(loads.start(s.tall.at[place], target))
-    for load, held, target in passing:
-        load.wait()
-        stores.append(loads.start(held, target))
     load_small.wait()
     load_bias.wait()
     part_width = s.small.shape[1]
@@ -918,14 +911,34 @@
         for part in range(parts):
             at = base + place * parts + part
             s.row[place : place + 1, part * part_width : (part + 1) * part_width] = s.small[at : at + 1]
-        target[...] = s.row[place : place + 1, :].reshape(width)
+        s.flat[place, :] = s.row[place : place + 1, :].reshape(width)
+        stores.append(loads.start(s.flat.at[place], target))
     base += 6 * parts + 8
     for place, target in enumerate((b_query, b_value)):
         at = base + 2 * place
         s.row[6:7, 0:part_width] = s.small[at : at + 1]
         s.row[6:7, part_width : 2 * part_width] = s.small[at + 1 : at + 2]
-        target[...] = s.row[6:7, 0:local].reshape(local)
+        s.half_flat[place, :] = s.row[6:7, 0:local].reshape(local)
+        stores.append(loads.start(s.half_flat.at[place], target))
     b_fc1[...] = s.bias[0:1, 0:rows].reshape(rows)
+    for pair in range(3):
+        load_attn[pair].wait()
+        at = slice(pair * LANES, (pair + 1) * LANES)
+        for place, target in enumerate((w_query, w_key, w_value)):
+            s.tall[place, :, at] = s.attn[1 + pair, :, place * LANES : (place + 1) * LANES].astype(F32)
+            stores.append(loads.start(s.tall.at[place, :, pl.ds(pair * LANES, LANES)], target.at[:, pl.ds(pair * LANES, LANES)]))
+    load_attn[3].wait()
+    s.wide[:, 0:local] = s.attn[0, 0:local].astype(F32)
+    s.wide[:, local : 2 * local] = s.attn[0, local : 2 * local].astype(F32)
+    stores.append(loads.start(s.wide, w_out))
+    for load, held, target in passing:
+        load.wait()
+        stores.append(loads.start(held, target))
+    if not whole_shards:
+        for source, held, target in ((fc1_in, s.fc1, w_fc1), (fc2_in, s.fc2, w_fc2)):
+            loads.start(source, held).wait()
+            s.cut[...] = held[0:rows]
+            loads.start(s.cut, target).wait()
     for copy in stores:
         copy.wait()
 
@@ -938,7 +951,7 @@
     rest_count = n // 16
     small_half = seq // 2
     part_width = 256
-    copies = 6 * ring + 4 * ring + 40 + 5 * (10 + rest_count)
+    copies = 11 * ring + 64 + 10 * 4 + 9 * (rest_count - 1)
     vmem = pltpu.VMEM
     shared = 2 * rows_per
     scratch = dict(
@@ -948,7 +961,7 @@
         b_all=vmem((slots, 8, LANES), F32),
         cot_all=vmem((4, seq, width), BF16),
         meta=vmem((2, 8, LANES), jnp.int32),
-        load_sems=pltpu.SemaphoreType.DMA((36,)),
+        load_sems=pltpu.SemaphoreType.DMA((39,)),
         kept=vmem((1, dims.patches), jnp.int32),
         tokens=vmem((1, dims.tok_rows, width), BF16),
         prompts=vmem((dims.prompt_rows, width), BF16),
@@ -1056,7 +1069,7 @@
     seq, width, local, rows = dims.seq, dims.width, dims.local, dims.rows
     vmem = pltpu.VMEM
     scratch = dict(
-        load_sems=pltpu.SemaphoreType.DMA((28,)),
+        load_sems=pltpu.SemaphoreType.DMA((36,)),
         attn=vmem((4, width, local), BF16),
         wide=vmem((local, width), F32),
         tall=vmem((3, width, local), F32),
@@ -1064,6 +1077,8 @@
         bias=vmem((8, LANES), F32),
         prompts=vmem((dims.prompt_rows, width), F32),
         row=vmem((8, width), F32),
+        flat=vmem((6, width), F32),
+        half_flat=vmem((2, local), F32),
         rows=vmem((1, seq, width), BF16),
         tok=vmem((dims.tok_rows, 1, width), F32),
         fc1=vmem((dims.rows_per, width), F32),
@@ -1087,7 +1102,7 @@
         functools.partial(finish_kernel, dims),
         out_shape=shapes,
         in_specs=[anywhere] * 7,
-        out_specs=[whole if len(shape.shape) == 1 else anywhere for shape in shapes],
+        out_specs=[whole if place == 15 else anywhere for place in range(len(shapes))],
         scratch_shapes=list(scratch.values()),
         compiler_params=pltpu.CompilerParams(vmem_limit_bytes=60 * 2**20),
     )(*results)

time: 119 us -> 114 us (0.958)
  Pallas kernels: 117 us -> 112 us
    pallas_call x1, Pallas kernels: 112 us -> 107 us  [layer(): pl.pallas_call(functools.partial(layer_kernel, dims), out_shape=(shape((1...]
where the time goes in v3:
time: 114 us; the launch traced here: 113 us
  Pallas kernels  112 us (98%)
  between operations  1.48 us (1%)
    pallas_call x1, Pallas kernels, layer(): pl.pallas_call(functools.partial(layer_kernel, dims), out_shape=(shape((1...  107 us
    pallas_call x1, Pallas kernels, finish(): pl.pallas_call(functools.partial(finish_kernel, dims), out_shape=shapes,...  4.67 us

profile of v3, /device:TPU:0, one launch (start us, length us, event | category | flops | bytes accessed | tf_op | source)
XLA Modules:
  0.0 113.5 jit_solution(8216043312137784709)
XLA Ops:
  1.3 107.3 %shard_map.331 = (bf16[1,256,768]{2,1,0:T(8,128)(2,1)}, f32[197,1,768]{2,1,0:T(1,128)}, bf16[4,768,384]{2,1,0:T(8,128)(2,1)}, f32[256,256]{1,0:T(8,128)}, f32[96...) custom-call(s32[1]{0:T(128)S(6)} %copy.38.refs_0_, bf16[1,197,768]{2,1,0:T(8,128)(2,1)} %refs_1_.1, ...), custom_call_target="tpu_custom_call" | custom-call | tf_op jit(solution)/shard_map/pallas_call | solution.py:1048
  108.6 4.7 %shard_map.332 = (bf16[1,256,768]{2,1,0:T(8,128)(2,1)}, f32[197,1,768]{2,1,0:T(1,128)}, f32[50,768]{1,0:T(8,128)}, f32[768]{0:T(1024)}, f32[768]{0:T(1024)}, /*i...) custom-call(bf16[1,256,768]{2,1,0:T(8,128)(2,1)} %get-tuple-element., ...), custom_call_target="tpu_custom_call" | custom-call | tf_op jit(solution)/shard_map/pallas_call | solution.py:1101

commit v4 on v3

--- a/solution.py
+++ b/solution.py
@@ -85,41 +85,88 @@
 )
 
 
+class Once:
+    def __init__(self, wait):
+        self.pending = wait
+
+    def wait(self):
+        if self.pending is not None:
+            self.pending()
+            self.pending = None
+
+
 class Loads:
-    def __init__(self, sems):
+    def __init__(self, sems, depth):
         self.sems = sems
-        self.count = 0
+        self.depth = depth
+        self.copies = []
+
+    def take(self):
+        place = len(self.copies)
+        if place >= self.depth:
+            self.copies[place - self.depth].wait()
+        return self.sems.at[place % self.depth]
 
     def start(self, source, target):
-        copy = pltpu.make_async_copy(source, target, self.sems.at[self.count])
+        copy = pltpu.make_async_copy(source, target, self.take())
         copy.start()
-        self.count += 1
-        return copy
+        self.copies.append(Once(copy.wait))
+        return self.copies[-1]
+
+    def start_parts(self, pieces, whole):
+        sem = self.take()
+        for source, target in pieces:
+            pltpu.make_async_copy(source, target, sem).start()
+        self.copies.append(Once(pltpu.make_async_copy(whole, whole, sem).wait))
+        return self.copies[-1]
 
 
 class Links:
-    def __init__(self, send_sems, recv_sems):
+    def __init__(self, send_sems, recv_sems, depth):
         self.send_sems = send_sems
         self.recv_sems = recv_sems
-        self.copies = []
-
-    def send(self, source, target, device):
-        place = len(self.copies)
+        self.depth = depth
+        self.sends = []
+        self.arrivals = 0
+
+    def copy(self, source, target, device, arrival):
+        place = len(self.sends)
+        if place >= self.depth:
+            self.sends[place - self.depth].wait()
         copy = pltpu.make_async_remote_copy(
             src_ref=source,
             dst_ref=target,
-            send_sem=self.send_sems.at[place],
-            recv_sem=self.recv_sems.at[place],
+            send_sem=self.send_sems.at[place % self.depth],
+            recv_sem=self.recv_sems.at[arrival],
             device_id=device,
             device_id_type=MESH,
         )
         copy.start()
-        self.copies.append(copy)
+        self.sends.append(Once(copy.wait_send))
         return copy
 
+    def send(self, source, target, device):
+        copy = self.copy(source, target, device, self.arrivals)
+        self.arrivals += 1
+        return copy
+
+    def send_parts(self, pieces, whole):
+        arrival = self.arrivals
+        self.arrivals += 1
+        for source, target, device in pieces:
+            self.copy(source, target, device, arrival)
+        return pltpu.make_async_remote_copy(
+            src_ref=whole,
+            dst_ref=whole,
+            send_sem=self.send_sems.at[0],
+            recv_sem=self.recv_sems.at[arrival],
+            device_id=device,
+            device_id_type=MESH,
+        )
+
     def drain(self):
-        for copy in self.copies:
-            copy.wait_send()
+        for copy in self.sends:
+            copy.wait()
 
 
 def layer_kernel(dims, *refs):
@@ -175,10 +222,10 @@
     for partner in partners:
         pl.semaphore_signal(barrier, inc=1, device_id=partner, device_id_type=MESH)
 
-    links = Links(s.send_sems, s.recv_sems)
+    links = Links(s.send_sems, s.recv_sems, dims.send_depth)
 
     w_all, b_all, cot_all = s.w_all, s.b_all, s.cot_all
-    loads = Loads(s.load_sems)
+    loads = Loads(s.load_sems, dims.load_depth)
     load_kept = loads.start(kept, s.kept)
     load_fc = [
         loads.start(fc1, w_all.at[0, pl.ds(0, rows_per)]),
@@ -187,15 +234,20 @@
     load_cot = loads.start(cot.at[0], cot_all.at[0])
     load_rows = [loads.start(tokens, s.tokens), loads.start(prompts, s.prompts)]
     load_vectors = [loads.start(ref, getattr(s, name)) for ref, name in zip(vectors_in, VECTORS)]
-    load_weights = [loads.start(weights_in[3], wout)]
-    for pair in range(pairs):
-        for place in range(3):
-            load_weights.append(
-                loads.start(
+    load_weights = [
+        loads.start(weights_in[3], wout),
+        loads.start_parts(
+            [
+                (
                     weights_in[place].at[:, pl.ds(pair * LANES, LANES)],
                     w_pair.at[pair, :, pl.ds(place * LANES, LANES)],
                 )
-            )
+                for pair in range(pairs)
+                for place in range(3)
+            ],
+            w_pair,
+        ),
+    ]
 
     limit = count_ref[0] + (1 + prompt_rows)
     src, pick = s.src, s.pick
@@ -689,20 +741,22 @@
         stages[1][item][0].wait_recv()
         mine = pl.ds(at_two, quarter)
         data[mine] = (data[mine].astype(F32) + two[...].astype(F32)).astype(data.dtype)
-        stages[2][item] = [
-            links.send(
-                data.at[pl.ds(pl.multiple_of(at_two + ((zq + hop) % 4) * leaf, leaf), leaf)],
-                by_z.at[hop - 1],
-                zdev[hop],
-            )
-            for hop in range(1, 4)
-        ]
+        stages[2][item] = links.send_parts(
+            [
+                (
+                    data.at[pl.ds(pl.multiple_of(at_two + ((zq + hop) % 4) * leaf, leaf), leaf)],
+                    by_z.at[hop - 1],
+                    zdev[hop],
+                )
+                for hop in range(1, 4)
+            ],
+            by_z,
+        )
 
     def spread_z(item):
         data, _, _, by_z, by_rest, done = items[item][:6]
         _, _, leaf, _, at_two = piece(item)
-        for copy in stages[2][item]:
-            copy.wait_recv()
+        stages[2][item].wait_recv()
         mine = pl.ds(pl.multiple_of(at_two + zq * leaf, leaf), leaf)
         total = data[mine].astype(F32)
         for hop in range(3):
@@ -719,15 +773,15 @@
             for owner in range(rest_count):
                 total += by_rest[(rest - owner + rest_count) % rest_count].astype(F32)
         done[mine] = total.astype(done.dtype)
-        stages[3][item] = [
-            links.send(done.at[mine], done.at[mine], zdev[hop]) for hop in range(1, 4)
-        ]
+        stages[3][item] = links.send_parts(
+            [(done.at[mine], done.at[mine], zdev[hop]) for hop in range(1, 4)],
+            done.at[pl.ds(0, 3 * leaf)],
+        )
 
     def spread_two(item):
         done = items[item][5]
         _, quarter, _, _, at_two = piece(item)
-        for copy in stages[3][item]:
-            copy.wait_recv()
+        stages[3][item].wait_recv()
         mine = pl.ds(at_two, quarter)
         stages[4][item] = [links.send(done.at[mine], done.at[mine], items[item][7][1])]
 
@@ -888,7 +942,7 @@
     s = SimpleNamespace(**dict(zip(dims.finish, it)))
     width, local = dims.width, dims.local
     rows = w_fc1.shape[0]
-    loads = Loads(s.load_sems)
+    loads = Loads(s.load_sems, dims.finish_depth)
     load_small = loads.start(small_in, s.small)
     load_bias = loads.start(bias_in, s.bias)
     load_attn = [loads.start(attn_in.at[array], s.attn.at[array]) for array in (1, 2, 3, 0)]
@@ -951,17 +1005,17 @@
     rest_count = n // 16
     small_half = seq // 2
     part_width = 256
-    copies = 11 * ring + 64 + 10 * 4 + 9 * (rest_count - 1)
+    arrivals = 11 * ring + 68 + 9 * (rest_count - 1)
     vmem = pltpu.VMEM
     shared = 2 * rows_per
     scratch = dict(
-        send_sems=pltpu.SemaphoreType.DMA((copies,)),
-        recv_sems=pltpu.SemaphoreType.DMA((copies,)),
+        send_sems=pltpu.SemaphoreType.DMA((dims.send_depth,)),
+        recv_sems=pltpu.SemaphoreType.DMA((arrivals,)),
         w_all=vmem((slots, shared, width), BF16),
         b_all=vmem((slots, 8, LANES), F32),
         cot_all=vmem((4, seq, width), BF16),
         meta=vmem((2, 8, LANES), jnp.int32),
-        load_sems=pltpu.SemaphoreType.DMA((39,)),
+        load_sems=pltpu.SemaphoreType.DMA((dims.load_depth,)),
         kept=vmem((1, dims.patches), jnp.int32),
         tokens=vmem((1, dims.tok_rows, width), BF16),
         prompts=vmem((dims.prompt_rows, width), BF16),
@@ -1069,7 +1123,7 @@
     seq, width, local, rows = dims.seq, dims.width, dims.local, dims.rows
     vmem = pltpu.VMEM
     scratch = dict(
-        load_sems=pltpu.SemaphoreType.DMA((36,)),
+        load_sems=pltpu.SemaphoreType.DMA((dims.finish_depth,)),
         attn=vmem((4, width, local), BF16),
         wide=vmem((local, width), F32),
         tall=vmem((3, width, local), F32),
@@ -1126,7 +1180,7 @@
         n=n, ring=ring, slots=slots, chunk_slots=chunk_slots, rows_per=rows_per, rows=rows, seq=seq,
         width=width, local=local, tok_rows=tok_rows, tok_pad=round_up(tok_rows, 16),
         prompt_rows=prompt_rows, prompt_pad=round_up(prompt_rows, 16),
-        patches=kept_index.shape[1],
+        patches=kept_index.shape[1], send_depth=32, load_depth=17, finish_depth=32,
     )
     if rows_per != rows:
         spare = ((0, rows_per - rows), (0, 0))

time: 114 us -> 112 us (0.982)
  Pallas kernels: 112 us -> 110 us
    pallas_call x1, Pallas kernels: 107 us -> 105 us  [layer(): pl.pallas_call(functools.partial(layer_kernel, dims), out_shape=(shape((1...]
where the time goes in v4:
time: 112 us
  Pallas kernels  110 us (98%)
  between operations  1.48 us (1%)
    pallas_call x1, Pallas kernels, layer(): pl.pallas_call(functools.partial(layer_kernel, dims), out_shape=(shape((1...  105 us
    pallas_call x1, Pallas kernels, finish(): pl.pallas_call(functools.partial(finish_kernel, dims), out_shape=shapes,...  4.64 us

profile of v4, /device:TPU:0, one launch (start us, length us, event | category | flops | bytes accessed | tf_op | source)
XLA Modules:
  0.0 111.5 jit_solution(16662295626774983483)
XLA Ops:
  1.3 105.4 %shard_map.331 = (bf16[1,256,768]{2,1,0:T(8,128)(2,1)}, f32[197,1,768]{2,1,0:T(1,128)}, bf16[4,768,384]{2,1,0:T(8,128)(2,1)}, f32[256,256]{1,0:T(8,128)}, f32[96...) custom-call(s32[1]{0:T(128)S(6)} %copy.38.refs_0_, bf16[1,197,768]{2,1,0:T(8,128)(2,1)} %refs_1_.1, ...), custom_call_target="tpu_custom_call" | custom-call | tf_op jit(solution)/shard_map/pallas_call | solution.py:1102
  106.7 4.6 %shard_map.332 = (bf16[1,256,768]{2,1,0:T(8,128)(2,1)}, f32[197,1,768]{2,1,0:T(1,128)}, f32[50,768]{1,0:T(8,128)}, f32[768]{0:T(1024)}, f32[768]{0:T(1024)}, /*i...) custom-call(bf16[1,256,768]{2,1,0:T(8,128)(2,1)} %get-tuple-element., ...), custom_call_target="tpu_custom_call" | custom-call | tf_op jit(solution)/shard_map/pallas_call | solution.py:1155

commit v5 on v4

--- a/solution.py
+++ b/solution.py
@@ -73,15 +73,15 @@
 )
 
 
-LATE_SUM = (8, 1)
+LATE_SUM = (8, 3)
 REDUCE_ORDER = (
     (0, 0), (-1, 0), (3, 0), (-2, 0), (5, 0), (1, 0), (-3, 0), (4, 0), (7, 0), (3, 1), (0, 1),
     (5, 1), (2, 0), (1, 1), (3, 2), (0, 2), (4, 1), (5, 2), (1, 2), (3, 3), (-4, 0), (7, 1),
     (6, 0), (0, 3), (1, 3), (7, 2), (4, 2), (2, 1), (3, 4), (-5, 0), (1, 4), (5, 3), (0, 4),
     (6, 1), (-6, 0), (7, 3), (2, 2), (-7, 0), (4, 3), (8, 0), (3, 5), (1, 5), (5, 4), (7, 4),
     (6, 2), (-8, 0), (8, 1), (2, 3), (0, 5), (6, 3), (5, 5), (4, 4), (8, 2), (2, 4), (7, 5),
-    (6, 4), (3, 6), (4, 5), (8, 3), (2, 5), (7, 6), (8, 4), (5, 6), (6, 5), (0, 6), (4, 6), (8, 5),
-    (6, 6), (1, 6), (2, 6), (8, 6),
+    (8, 3), (6, 4), (3, 6), (4, 5), (2, 5), (8, 4), (7, 6), (5, 6), (6, 5), (8, 5), (0, 6), (4, 6),
+    (8, 6), (6, 6), (1, 6), (2, 6),
 )
 
 
@@ -128,6 +128,7 @@
         self.depth = depth
         self.sends = []
         self.arrivals = 0
+        self.spare = []
 
     def copy(self, source, target, device, arrival):
         place = len(self.sends)
@@ -145,7 +146,9 @@
         self.sends.append(Once(copy.wait_send))
         return copy
 
-    def send(self, source, target, device):
+    def send(self, source, target, device, again=False):
+        if again and self.spare:
+            return self.copy(source, target, device, self.spare.pop(0))
         copy = self.copy(source, target, device, self.arrivals)
         self.arrivals += 1
         return copy
@@ -588,6 +591,7 @@
     bias_total = feed(0, (2,), bias_total)
     n2_far.wait_recv()
     bias_total = feed(0, (3,), bias_total)
+    early = links.arrivals
     feed_weights(0, bias_total)
     sum_b_step(1)
     for distance in range(1, chunk_slots // 2):
@@ -723,7 +727,7 @@
         half, _, _, _, _ = piece(item)
         device, _, p_one, _ = items[item][7]
         other = pl.ds(pl.multiple_of((1 - p_one) * half, half), half)
-        stages[0][item] = [links.send(data.at[other], one, device)]
+        stages[0][item] = [links.send(data.at[other], one, device, again=True)]
 
     def reduce_two(item):
         data, one, two = items[item][:3]
@@ -733,7 +737,7 @@
         data[mine] = (data[mine].astype(F32) + one[...].astype(F32)).astype(data.dtype)
         _, device, _, p_two = items[item][7]
         other = pl.ds(pl.multiple_of(at_one + (1 - p_two) * quarter, quarter), quarter)
-        stages[1][item] = [links.send(data.at[other], two, device)]
+        stages[1][item] = [links.send(data.at[other], two, device, again=True)]
 
     def reduce_z(item):
         data, _, two, by_z = items[item][:4]
@@ -783,14 +787,14 @@
         _, quarter, _, _, at_two = piece(item)
         stages[3][item].wait_recv()
         mine = pl.ds(at_two, quarter)
-        stages[4][item] = [links.send(done.at[mine], done.at[mine], items[item][7][1])]
+        stages[4][item] = [links.send(done.at[mine], done.at[mine], items[item][7][1], again=True)]
 
     def spread_one(item):
         done = items[item][5]
         half, _, _, at_one, _ = piece(item)
         stages[4][item][0].wait_recv()
         mine = pl.ds(at_one, half)
-        stages[5][item] = [links.send(done.at[mine], done.at[mine], items[item][7][0])]
+        stages[5][item] = [links.send(done.at[mine], done.at[mine], items[item][7][0], again=True)]
 
     def finish(item):
         stages[5][item][0].wait_recv()
@@ -804,6 +808,7 @@
             s.mixed_t[1], grad_branch[1, :, at]
         )
         ar[0, at, :] = total.astype(BF16)
+    links.spare = list(range(early))
     def out_back():
         part_sib[1, 1].wait_recv()
         cross[1].wait_recv()
@@ -848,7 +853,6 @@
             return (totals[0] + fold_rows(grads * unit_rows), totals[1] + fold_rows(grads))
 
         held.sums = lax.fori_loop(0, blocks, in_back, (empty,) * 2, unroll=4)
-        sum_a_until(ring)
 
     theirs = pl.ds(pl.multiple_of((1 - h) * small_half, small_half), small_half)
     ours = pl.ds(pl.multiple_of(h * small_half, small_half), small_half)
@@ -898,11 +902,18 @@
                 small_ref[at : at + 1, :] = chosen[:, 0:part_width]
                 small_ref[at + 1 : at + 2, 0 : local - part_width] = chosen[:, part_width:local]
         held.small_sib = links.send(small_ref.at[theirs], s.small_in.at[1], sib)
+        sum_a_until(ring)
         sum_b_until(ring)
 
     def reduce_small():
         held.small_sib.wait_recv()
         small_own[...] = small_ref[ours] + s.small_in[1]
+
+    final = s.small_out
+
+    def hand_small():
+        final[ours] = s.small_all[...]
+        held.small_back = links.send(s.small_all, s.small_in.at[0], sib)
 
     blocks_beside = [
         functools.partial(pair_back, 0), functools.partial(pair_back, 1), functools.partial(pair_back, 2),
@@ -918,10 +929,9 @@
             steps[stage](item)
             if (item, stage) == LATE_SUM:
                 sum_b_end()
-    final = s.small_out
-    final[ours] = s.small_all[...]
-    small_back = links.send(s.small_all, s.small_in.at[0], sib)
-    small_back.wait_recv()
+            if (item, stage) == (len(cuts), len(steps) - 1):
+                hand_small()
+    held.small_back.wait_recv()
     final[theirs] = s.small_in[0]
     final[small_base + 8 : small_base + 12, :] = jnp.where(
         h == 0, final[small_base : small_base + 4, :], final[small_base + 4 : small_base + 8, :]
@@ -943,15 +953,28 @@
     width, local = dims.width, dims.local
     rows = w_fc1.shape[0]
     loads = Loads(s.load_sems, dims.finish_depth)
-    load_small = loads.start(small_in, s.small)
-    load_bias = loads.start(bias_in, s.bias)
-    load_attn = [loads.start(attn_in.at[array], s.attn.at[array]) for array in (1, 2, 3, 0)]
-    passing = [(rows_in, s.rows, layer_out), (tok_in, s.tok, grad_tokens)]
     whole_shards = rows == fc1_in.shape[0]
+    passing = [(tok_in, s.tok, grad_tokens), (rows_in, s.rows, layer_out)]
     if whole_shards:
         passing += [(fc1_in, s.fc1, w_fc1), (fc2_in, s.fc2, w_fc2)]
     passing = [(loads.start(source, held), held, target) for source, held, target in passing]
+    load_attn = [loads.start(attn_in.at[array], s.attn.at[array]) for array in (1, 2, 3, 0)]
+    load_small = loads.start(small_in, s.small)
+    load_bias = loads.start(bias_in, s.bias)
     stores = []
+    for load, held, target in passing:
+        load.wait()
+        stores.append(loads.start(held, target))
+    for pair in range(3):
+        load_attn[pair].wait()
+        at = slice(pair * LANES, (pair + 1) * LANES)
+        for place, target in enumerate((w_query, w_key, w_value)):
+            s.tall[place, :, at] = s.attn[1 + pair, :, place * LANES : (place + 1) * LANES].astype(F32)
+            stores.append(loads.start(s.tall.at[place, :, pl.ds(pair * LANES, LANES)], target.at[:, pl.ds(pair * LANES, LANES)]))
+    load_attn[3].wait()
+    s.wide[:, 0:local] = s.attn[0, 0:local].astype(F32)
+    s.wide[:, local : 2 * local] = s.attn[0, local : 2 * local].astype(F32)
+    stores.append(loads.start(s.wide, w_out))
     load_small.wait()
     load_bias.wait()
     part_width = s.small.shape[1]
@@ -975,19 +998,6 @@
         s.half_flat[place, :] = s.row[6:7, 0:local].reshape(local)
         stores.append(loads.start(s.half_flat.at[place], target))
     b_fc1[...] = s.bias[0:1, 0:rows].reshape(rows)
-    for pair in range(3):
-        load_attn[pair].wait()
-        at = slice(pair * LANES, (pair + 1) * LANES)
-        for place, target in enumerate((w_query, w_key, w_value)):
-            s.tall[place, :, at] = s.attn[1 + pair, :, place * LANES : (place + 1) * LANES].astype(F32)
-            stores.append(loads.start(s.tall.at[place, :, pl.ds(pair * LANES, LANES)], target.at[:, pl.ds(pair * LANES, LANES)]))
-    load_attn[3].wait()
-    s.wide[:, 0:local] = s.attn[0, 0:local].astype(F32)
-    s.wide[:, local : 2 * local] = s.attn[0, local : 2 * local].astype(F32)
-    stores.append(loads.start(s.wide, w_out))
-    for load, held, target in passing:
-        load.wait()
-        stores.append(loads.start(held, target))
     if not whole_shards:
         for source, held, target in ((fc1_in, s.fc1, w_fc1), (fc2_in, s.fc2, w_fc2)):
             loads.start(source, held).wait()
@@ -1005,7 +1015,7 @@
     rest_count = n // 16
     small_half = seq // 2
     part_width = 256
-    arrivals = 11 * ring + 68 + 9 * (rest_count - 1)
+    arrivals = 11 * ring + 68 + 9 * (rest_count - 1) - min(36, 6 * ring + 6)
     vmem = pltpu.VMEM
     shared = 2 * rows_per
     scratch = dict(

time: 112 us -> 111 us (level)
  no operation moved by 1% of the time
where the time goes in v5:
time: 111 us
  Pallas kernels  110 us (99%)
  between operations  1.48 us (1%)
    pallas_call x1, Pallas kernels, layer(): pl.pallas_call(functools.partial(layer_kernel, dims), out_shape=(shape((1...  105 us
    pallas_call x1, Pallas kernels, finish(): pl.pallas_call(functools.partial(finish_kernel, dims), out_shape=shapes,...  4.58 us

profile of v5, /device:TPU:0, one launch (start us, length us, event | category | flops | bytes accessed | tf_op | source)
XLA Modules:
  0.0 111.2 jit_solution(8351291345812898526)
XLA Ops:
  1.3 105.1 %shard_map.331 = (bf16[1,256,768]{2,1,0:T(8,128)(2,1)}, f32[197,1,768]{2,1,0:T(1,128)}, bf16[4,768,384]{2,1,0:T(8,128)(2,1)}, f32[256,256]{1,0:T(8,128)}, f32[96...) custom-call(s32[1]{0:T(128)S(6)} %copy.38.refs_0_, bf16[1,197,768]{2,1,0:T(8,128)(2,1)} %refs_1_.1, ...), custom_call_target="tpu_custom_call" | custom-call | tf_op jit(solution)/shard_map/pallas_call | solution.py:1112
  106.4 4.6 %shard_map.332 = (bf16[1,256,768]{2,1,0:T(8,128)(2,1)}, f32[197,1,768]{2,1,0:T(1,128)}, f32[50,768]{1,0:T(8,128)}, f32[768]{0:T(1024)}, f32[768]{0:T(1024)}, /*i...) custom-call(bf16[1,256,768]{2,1,0:T(8,128)(2,1)} %get-tuple-element., ...), custom_call_target="tpu_custom_call" | custom-call | tf_op jit(solution)/shard_map/pallas_call | solution.py:1165

commit v6 on v5

--- a/solution.py
+++ b/solution.py
@@ -129,6 +129,9 @@
         self.sends = []
         self.arrivals = 0
         self.spare = []
+        self.clock = 0
+        self.heard = 0
+        self.group_spare = []
 
     def copy(self, source, target, device, arrival):
         place = len(self.sends)
@@ -154,18 +157,33 @@
         return copy
 
     def send_parts(self, pieces, whole):
-        arrival = self.arrivals
-        self.arrivals += 1
+        self.clock += 1
+        sent = self.clock
+        ready = [entry for entry in self.group_spare if entry[0] < self.heard]
+        if ready:
+            self.group_spare.remove(ready[0])
+            arrival = ready[0][1]
+        else:
+            arrival = self.arrivals
+            self.arrivals += 1
         for source, target, device in pieces:
             self.copy(source, target, device, arrival)
-        return pltpu.make_async_remote_copy(
+        wait = pltpu.make_async_remote_copy(
             src_ref=whole,
             dst_ref=whole,
             send_sem=self.send_sems.at[0],
             recv_sem=self.recv_sems.at[arrival],
             device_id=device,
             device_id_type=MESH,
-        )
+        ).wait_recv
+
+        def heard():
+            wait()
+            self.clock += 1
+            self.heard = max(self.heard, sent)
+            self.group_spare.append((self.clock, arrival))
+
+        return SimpleNamespace(wait_recv=heard)
 
     def drain(self):
         for copy in self.sends:
@@ -1015,7 +1033,7 @@
     rest_count = n // 16
     small_half = seq // 2
     part_width = 256
-    arrivals = 11 * ring + 68 + 9 * (rest_count - 1) - min(36, 6 * ring + 6)
+    arrivals = 11 * ring + 68 + 9 * (rest_count - 1) - min(36, 6 * ring + 6) - 8
     vmem = pltpu.VMEM
     shared = 2 * rows_per
     scratch = dict(

time: 111 us -> 111 us (level)
  no operation moved by 1% of the time
where the time goes in v6:
time: 111 us
  Pallas kernels  110 us (99%)
  between operations  1.48 us (1%)
    pallas_call x1, Pallas kernels, layer(): pl.pallas_call(functools.partial(layer_kernel, dims), out_shape=(shape((1...  105 us
    pallas_call x1, Pallas kernels, finish(): pl.pallas_call(functools.partial(finish_kernel, dims), out_shape=shapes,...  4.58 us

profile of v6, /device:TPU:0, one launch (start us, length us, event | category | flops | bytes accessed | tf_op | source)
XLA Modules:
  0.0 111.1 jit_solution(12012928787384370264)
XLA Ops:
  1.3 105.0 %shard_map.331 = (bf16[1,256,768]{2,1,0:T(8,128)(2,1)}, f32[197,1,768]{2,1,0:T(1,128)}, bf16[4,768,384]{2,1,0:T(8,128)(2,1)}, f32[256,256]{1,0:T(8,128)}, f32[96...) custom-call(s32[1]{0:T(128)S(6)} %copy.38.refs_0_, bf16[1,197,768]{2,1,0:T(8,128)(2,1)} %refs_1_.1, ...), custom_call_target="tpu_custom_call" | custom-call | tf_op jit(solution)/shard_map/pallas_call | solution.py:1130
  106.4 4.6 %shard_map.332 = (bf16[1,256,768]{2,1,0:T(8,128)(2,1)}, f32[197,1,768]{2,1,0:T(1,128)}, f32[50,768]{1,0:T(8,128)}, f32[768]{0:T(1024)}, f32[768]{0:T(1024)}, /*i...) custom-call(bf16[1,256,768]{2,1,0:T(8,128)(2,1)} %get-tuple-element., ...), custom_call_target="tpu_custom_call" | custom-call | tf_op jit(solution)/shard_map/pallas_call | solution.py:1183
